TPU v7x, 32 devices: a whole 2x2x4 slice. The times are simulated.
32 devices in a mesh: brick: 4 (over y, x), section: 2 (over core), dp: 4 (over z).
Axes of the slice: x: 2, y: 2, z: 4, core: 2. Of those that a mesh axis runs over, the one named last changes fastest.
Arguments:
- features: bfloat16 [2, 4, 16, 512, 128], P('section', 'dp', 'brick'), may hold values from -6 to 6
- weights: bfloat16 [2, 27, 128, 128], P('section'), may hold values from -0.109375 to 0.109375
- projection: bfloat16 [128, 128], replicated, may hold values from -0.5 to 0.5
- cotangent: bfloat16 [2, 4, 16, 512, 128], P('section', 'dp', 'brick'), may hold values from -0.078125 to 0.078125
- neighbours: int32 [2, 4, 16, 6], P('section', 'dp', 'brick'), may hold values from -1 to 15, as said below
- route: int32 [4, 16], P('dp', 'brick'), may hold values from 0 to 15, as said below
Outputs:
- activations: bfloat16 [2, 4, 16, 512, 128], P('section', 'dp', 'brick')
- weight_grads: float32 [2, 27, 128, 128], P('section')
- projection_grad: float32 [128, 128], replicated
Inputs may be any that keep to these rules, and one draw needn't show every extreme that they name: `neighbours`: owners hold 4 consecutive rows each. Entries 2 to 5 name bricks of the same owner; entry 0 names a brick of the same or the next owner, entry 1 of the same or the previous owner. `route`: each scene's row is a permutation of its bricks; every decoder owner receives 4 bricks; the bricks of one encoder owner go to at most 2 rows of one decoder owner, and every encoder owner sends exactly 2 to some decoder owner.
All inputs are finite; a program needn't handle non-finite values.
Results may differ from a plain program's by a relative error of at most 0.0059.
Values may be sent and summed in bfloat16 or wider, within the bound.
A program may use at most 128 MiB of HBM per device.

v0:
```python
import jax
import jax.numpy as jnp
from jax import lax
from jax.sharding import PartitionSpec as P

tap_moves = tuple(
    (
        (move_a, move_b, move_c)
        for move_a in (-1, 0, 1)
        for move_b in (-1, 0, 1)
        for move_c in (-1, 0, 1)
    )
)
source_part = {-1: slice(7, 8), 0: slice(0, 8), 1: slice(0, 1)}


def padded_2(shard, sides, width):
    for axis, dim in sides:
        size, length = (lax.axis_size(axis), shard.shape[dim])
        up = [(i, (i + 1) % size) for i in range(size - 1)]
        down = [(j, i) for i, j in up]
        last = lax.slice_in_dim(shard, length - width, length, axis=dim)
        initial = lax.slice_in_dim(shard, 0, width, axis=dim)
        before = lax.ppermute(last, axis, up)
        after = lax.ppermute(initial, axis, down)
        shard = jnp.concatenate([before, shard, after], axis=dim)
    return shard


def passed_along(block, axis, distance):
    devices = range(lax.axis_size(axis))
    route = [(i - distance, i) for i in devices if i - distance in devices]
    return lax.ppermute(block, axis, route)


def silu_slope(values):
    sigmoid_part = jax.nn.sigmoid(values)
    return sigmoid_part * (1.0 + values * (1.0 - sigmoid_part))


def pad_local(bricks_grid, neighbour_rows, after_lower, before_upper, owner_start):
    bricks_here = bricks_grid.shape[0]
    channels = bricks_grid.shape[-1]
    linkage = jnp.where(neighbour_rows >= 0, neighbour_rows - owner_start, bricks_here)
    linkage = jnp.concatenate([linkage, jnp.full((1, 6), bricks_here, jnp.int32)], 0)
    global_links = jnp.concatenate([neighbour_rows, jnp.full((1, 6), -1, jnp.int32)], 0)
    empty_plane = jnp.zeros((1, 8, 8, channels), bricks_grid.dtype)
    plus_table = jnp.concatenate([bricks_grid[:, 0], after_lower, empty_plane], 0)
    minus_table = jnp.concatenate([bricks_grid[:, 7], before_upper, empty_plane], 0)
    blocks = {}
    for tap_move in tap_moves:
        step_a, step_b, step_c = tap_move
        if step_a == 0 and step_b == 0 and (step_c == 0):
            blocks[tap_move] = bricks_grid
            continue
        chain_rows = jnp.arange(bricks_here, dtype=jnp.int32)
        if step_c != 0:
            chain_rows = linkage[chain_rows, 4 if step_c > 0 else 5]
        if step_b != 0:
            chain_rows = linkage[chain_rows, 2 if step_b > 0 else 3]
        if step_a == 0:
            region = bricks_grid[:, :, source_part[step_b], source_part[step_c]]
            region = jnp.concatenate(
                [region, jnp.zeros((1,) + region.shape[1:], bricks_grid.dtype)], 0
            )
            filling = region[chain_rows]
        else:
            far_rows = global_links[chain_rows, 0 if step_a > 0 else 1]
            relative = far_rows - owner_start
            if step_a > 0:
                plane_table = plus_table
                index_rows = jnp.where(far_rows >= 0, relative, 2 * bricks_here)
            else:
                plane_table = minus_table
                index_rows = jnp.where(
                    far_rows >= 0,
                    jnp.where(relative >= 0, relative, relative + 2 * bricks_here),
                    2 * bricks_here,
                )
            filling = plane_table[:, source_part[step_b], source_part[step_c]][index_rows][:, None]
        blocks[tap_move] = filling
    slabs = []
    for step_a in (-1, 0, 1):
        lines = []
        for step_b in (-1, 0, 1):
            lines.append(
                jnp.concatenate([blocks[step_a, step_b, step_c] for step_c in (-1, 0, 1)], 3)
            )
        slabs.append(jnp.concatenate(lines, 2))
    return jnp.concatenate(slabs, 1)


def group_block(padded, move_a, move_b):
    start_a, start_b = (move_a + 1, move_b + 1)
    parts = [
        padded[:, start_a : start_a + 8, start_b : start_b + 8, start_c : start_c + 8]
        for start_c in (0, 1, 2)
    ]
    joined = jnp.concatenate(parts, -1)
    return joined.reshape(-1, joined.shape[-1])


def apply_taps(padded, section_weights):
    channels = section_weights.shape[-1]
    summed = jnp.zeros((padded.shape[0] * 512, channels), jnp.float32)
    for move_a in (-1, 0, 1):
        for move_b in (-1, 0, 1):
            first = 9 * (move_a + 1) + 3 * (move_b + 1)
            stacked_weights = section_weights[first : first + 3].reshape(3 * channels, channels)
            summed = summed + jnp.dot(
                group_block(padded, move_a, move_b),
                stacked_weights,
                preferred_element_type=jnp.float32,
            )
    return summed


def tap_gradients(padded, slope_rows):
    channels = slope_rows.shape[-1]
    groups_out = []
    for move_a in (-1, 0, 1):
        for move_b in (-1, 0, 1):
            product = lax.dot_general(
                group_block(padded, move_a, move_b),
                slope_rows,
                (((0,), (0,)), ((), ())),
                preferred_element_type=jnp.float32,
            )
            groups_out.append(product.reshape(3, channels, channels))
    return jnp.concatenate(groups_out, 0)


def slot_positions(owner_group, groups, capacity):
    onehot = (owner_group[:, None] == jnp.arange(groups, dtype=jnp.int32)[None, :]).astype(
        jnp.int32
    )
    earlier = jnp.cumsum(onehot, 0) - onehot
    return owner_group * capacity + jnp.sum(earlier * onehot, 1)


def pack_slots(rows, slot_index, labels, slots_total):
    bricks_here = rows.shape[0]
    picked = (
        jnp.full((slots_total,), bricks_here, jnp.int32)
        .at[slot_index]
        .set(jnp.arange(bricks_here, dtype=jnp.int32))
    )
    padded_rows = jnp.concatenate([rows, jnp.zeros((1,) + rows.shape[1:], rows.dtype)], 0)
    tagged = jnp.full((slots_total,), bricks_here, jnp.int32).at[slot_index].set(labels)
    return (padded_rows[picked], tagged)


def unpack_slots(received, tags, bricks_here):
    chosen = (
        jnp.zeros((bricks_here,), jnp.int32)
        .at[tags]
        .set(jnp.arange(tags.shape[0], dtype=jnp.int32), mode="drop")
    )
    return received[chosen]


def pack_back(rows, tags):
    padded_rows = jnp.concatenate([rows, jnp.zeros((1,) + rows.shape[1:], rows.dtype)], 0)
    return padded_rows[tags]


def body(features, weights, projection, cotangent, neighbours, route):
    local_rows = features[0, 0]
    bricks_here = local_rows.shape[0]
    channels = local_rows.shape[-1]
    bricks_grid = local_rows.reshape(bricks_here, 8, 8, 8, channels)
    owner_start = lax.axis_index("brick") * bricks_here
    lower_planes = bricks_grid[:, 0]
    upper_planes = bricks_grid[:, 7]
    stacked = jnp.stack([lower_planes, upper_planes], 1)
    extended = padded_2(stacked, (("brick", 0),), bricks_here)
    after_lower = extended[2 * bricks_here :, 0]
    before_upper = extended[:bricks_here, 1]
    padded = pad_local(bricks_grid, neighbours[0, 0], after_lower, before_upper, owner_start)
    section_taps = apply_taps(padded, weights[0])
    skip_tiles = jax.nn.silu(section_taps).astype(jnp.bfloat16).reshape(bricks_here, 512, channels)
    devices_brick = lax.axis_size("brick")
    capacity = max(2, 3 * bricks_here // (2 * devices_brick))
    target_owner = route[0] // bricks_here
    target_offset = route[0] % bricks_here
    slot_index = slot_positions(target_owner, devices_brick, capacity)
    buffer_rows, tags = pack_slots(skip_tiles, slot_index, target_offset, devices_brick * capacity)
    received, received_tags = (
        lax.all_to_all(buffer_rows, "brick", split_axis=0, concat_axis=0, tiled=True),
        lax.all_to_all(tags, "brick", split_axis=0, concat_axis=0, tiled=True),
    )
    arranged = unpack_slots(received, received_tags, bricks_here)
    skip_rows = passed_along(arranged, "section", 1)
    skip_flat = skip_rows.reshape(-1, channels)
    section_input = section_taps + jnp.dot(
        skip_flat, projection, preferred_element_type=jnp.float32
    )
    section_output = jax.nn.silu(section_input).astype(jnp.bfloat16)
    cotangent_rows = cotangent[0, 0].reshape(-1, channels).astype(jnp.float32)
    slope_factor = silu_slope(section_input)
    first_slope = (cotangent_rows * slope_factor).astype(jnp.bfloat16)
    skip_grad = (
        jnp.dot(first_slope, projection.T, preferred_element_type=jnp.float32)
        .astype(jnp.bfloat16)
        .reshape(bricks_here, 512, channels)
    )
    lowered = passed_along(skip_grad, "section", -1)
    returned = lax.all_to_all(
        pack_back(lowered, received_tags), "brick", split_axis=0, concat_axis=0, tiled=True
    )
    back_rows = returned[slot_index]
    final_slope = (
        (cotangent_rows + back_rows.reshape(-1, channels).astype(jnp.float32)) * slope_factor
    ).astype(jnp.bfloat16)
    local_taps = tap_gradients(padded, final_slope)
    local_projection = lax.dot_general(
        skip_flat, final_slope, (((0,), (0,)), ((), ())), preferred_element_type=jnp.float32
    )
    weight_sum = lax.psum(local_taps, ("brick", "dp"))
    partial_projection = lax.psum(local_projection, ("brick", "dp"))
    projection_sum = lax.psum(partial_projection, "section")
    return (
        section_output.reshape(1, 1, bricks_here, 512, channels),
        weight_sum[None],
        projection_sum,
    )


def solution(mesh):
    return jax.shard_map(
        body,
        mesh=mesh,
        in_specs=(
            P("section", "dp", "brick", None, None),
            P("section", None, None, None),
            P(),
            P("section", "dp", "brick", None, None),
            P("section", "dp", "brick", None),
            P("dp", "brick"),
        ),
        out_specs=(P("section", "dp", "brick", None, None), P("section", None, None, None), P()),
        check_vma=False,
    )
```

profile of v0, /device:TPU:0, one launch (start us, length us, event | category | flops | bytes accessed | tf_op | source)
XLA Modules:
  0.0 356.5 jit_solution(7548089026313140224)
XLA Ops:
  11.4 6.1 %collective-permute-start = (bf16[4,2,8,8,128]{4,0,3,2,1:T(4,128)(2,1)}, bf16[4,2,8,8,128]{4,0,3,2,1:T(4,128)(2,1)}, u32[]{:S(2)}, u32[]{:S(2)}) collective-permute-start(bf16[4,2,8,8,128]{4,0,3,2,1:T(4,128)(2,1)} %pad_maximum_fusion.12), channel_id=1, source_target_pairs={{0,8},{8,16},{16,24},{1,9},{9,17},{17,25},{2,10},{10,18},{18,26},{... | collective-permute-start | bytes 393224 | tf_op jit(solution)/shard_map/ppermute | solution.py:24
  19.2 3.7 %all-to-all-start.1 = ((s32[4,2,1]{1,2,0:T(1,128)}), s32[4,2,1]{1,2,0:T(1,128)}, u32[]{:S(2)}, u32[]{:S(2)}) async-start(s32[4,2,1]{1,2,0:T(1,128)} %bitcast.162), calls=%async_computation.1 | async-start | bytes 4096 | tf_op jit(solution)/shard_map/all_to_all | solution.py:190
  60.4 2.2 fusion.70
  62.6 2.1 pad_maximum_fusion.5
  79.7 1.6 gather_fusion.43
  86.8 5.2 %maximum_maximum_fusion.1 = bf16[4,9,10,10,128]{4,0,3,2,1:T(4,128)(2,1)S(1)} fusion(bf16[4,1,1,1,128]{4,0,3,2,1:T(4,128)(2,1)S(1)} %bitcast.641, bf16[4,1,1,8,128]{4,0,3,2,1:T(4,128)(2,1)S(1)} %bitcast.629, bf16[4,1,1,1,128]{4,0,3,2,1:T(4,128)(2,1)S(1)} %bitcast.639, bf16[4,1,8,1,128]{4,0,3,2,1:T(4,128)(2,1)S(1)} %bitcast.627, ...), kind=kLoop, calls=%fused_computation.97 | loop fusion | flops 7833600 | bytes 1843200 | tf_op jit(solution)/shard_map/concatenate | solution.py:90
  92.0 2.6 fusion.68
  108.5 2.5 maximum_maximum_fusion
  111.0 2.3 fusion.69
  127.1 1.6 multiply_convert_fusion.1
  128.8 1.8 gather_fusion.52
  130.6 4.1 %all-to-all-start = ((bf16[8,512,128]{2,1,0:T(8,128)(2,1)}), bf16[8,512,128]{2,1,0:T(8,128)(2,1)S(1)}, u32[]{:S(2)}, u32[]{:S(2)}) async-start(bf16[8,512,128]{2,1,0:T(8,128)(2,1)} %gather_fusion.52), calls=%async_computation | async-start | bytes 2097152 | tf_op jit(solution)/shard_map/all_to_all | solution.py:189
  137.3 10.8 %all-to-all-done = bf16[8,512,128]{2,1,0:T(8,128)(2,1)S(1)} async-done(((bf16[8,512,128]{2,1,0:T(8,128)(2,1)}), bf16[8,512,128]{2,1,0:T(8,128)(2,1)S(1)}, u32[]{:S(2)}, u32[]{:S(2)}) %all-to-all-start) | async-done | bytes 1048608 | tf_op jit(solution)/shard_map/all_to_all | solution.py:189
  150.9 1.7 collective-permute-done.2
  153.4 1.5 convolution_add_fusion
  157.2 2.5 collective-permute-done.3
  159.8 1.7 gather_fusion.54
  161.4 4.2 %all-to-all-start.2 = ((bf16[8,512,128]{2,1,0:T(8,128)(2,1)}), bf16[8,512,128]{2,1,0:T(8,128)(2,1)}, u32[]{:S(2)}, u32[]{:S(2)}) async-start(bf16[8,512,128]{2,1,0:T(8,128)(2,1)} %gather_fusion.54), calls=%async_computation.2 | async-start | bytes 2097152 | tf_op jit(solution)/shard_map/all_to_all | solution.py:208
  165.7 2.9 copy.180
  170.0 2.6 copy.181
  172.6 1.7 copy.182
  174.3 2.6 copy.177
  176.9 2.7 copy.178
  179.6 1.7 copy.179
  181.3 2.7 copy.183
  184.0 1.7 copy.184
  185.7 1.8 copy.185
  187.5 2.6 gather_fusion.55
  190.2 2.7 fusion.2
  203.2 123.6 %all-reduce.38.cloned.1.call-done = (f32[1,27,128,128]{3,2,1,0:T(8,128)}, f32[128,128]{1,0:T(8,128)}) async-done(((f32[1,27,128,128]{3,2,1,0:T(8,128)}, f32[128,128]{1,0:T(8,128)}), (f32[1,27,128,128]{3,2,1,0:T(8,128)}, f32[128,128]{1,0:T(8,128)})) %all-reduce.38.cloned.1.call-update) | async-done | bytes 1835024 | tf_op jit(solution)/shard_map/psum | solution.py:219
  326.8 19.3 %all-reduce.36.cloned.1.call-done = f32[128,128]{1,0:T(8,128)} async-done(((f32[128,128]{1,0:T(8,128)}), f32[128,128]{1,0:T(8,128)}) %all-reduce.36.cloned.1.call-update) | async-done | bytes 65552 | tf_op jit(solution)/shard_map/psum | solution.py:221
  346.1 2.9 copy.233
  (352 shorter events, 111.3 us)
Async XLA Ops:
  7.2 146.2 %copy-start = (bf16[128,128]{1,0:T(8,128)(2,1)S(1)}, bf16[128,128]{1,0:T(8,128)(2,1)}, u32[]{:S(2)}) copy-start(bf16[128,128]{1,0:T(8,128)(2,1)} %param.8) | copy-start | bytes 98308
  7.2 15.9 %copy-start.59 = (s32[4]{0:T(128)S(1)}, s32[4]{0:T(128)}, u32[]{:S(2)}) copy-start(s32[4]{0:T(128)} %constant.519) | copy-start | bytes 52
  7.2 17.2 %copy-start.58 = (s32[4]{0:T(128)S(1)}, s32[4]{0:T(128)}, u32[]{:S(2)}) copy-start(s32[4]{0:T(128)} %constant.497) | copy-start | bytes 52
  7.2 10.4 %copy-start.63 = (s32[1,4]{1,0:T(1,128)S(1)}, s32[1,4]{1,0:T(1,128)}, u32[]{:S(2)}) copy-start(s32[1,4]{1,0:T(1,128)} %param.11) | copy-start | bytes 52
  7.2 15.8 %copy-start.60 = (s32[1,1,4,6]{3,2,1,0:T(4,128)S(1)}, s32[1,1,4,6]{3,2,1,0:T(4,128)}, u32[]{:S(2)}) copy-start(s32[1,1,4,6]{3,2,1,0:T(4,128)} %param.10) | copy-start | bytes 292
  10.2 59.7 %collective-permute-start.1 = (bf16[4,2,8,8,128]{4,0,3,2,1:T(4,128)(2,1)}, bf16[4,2,8,8,128]{4,0,3,2,1:T(4,128)(2,1)}, u32[]{:S(2)}, u32[]{:S(2)}) collective-permute-start(bf16[4,2,8,8,128]{4,0,3,2,1:T(4,128)(2,1)} %pad_maximum_fusion.12), channel_id=1, source_target_pairs={{8,0},{16,8},{24,16},{9,1},{17,9},{25,17},{10,2},{18,10},{26,18},{... | collective-permute-start | bytes 393224 | tf_op jit(solution)/shard_map/ppermute | solution.py:25
  11.4 59.3 %collective-permute-start = (bf16[4,2,8,8,128]{4,0,3,2,1:T(4,128)(2,1)}, bf16[4,2,8,8,128]{4,0,3,2,1:T(4,128)(2,1)}, u32[]{:S(2)}, u32[]{:S(2)}) collective-permute-start(bf16[4,2,8,8,128]{4,0,3,2,1:T(4,128)(2,1)} %pad_maximum_fusion.12), channel_id=1, source_target_pairs={{0,8},{8,16},{16,24},{1,9},{9,17},{17,25},{2,10},{10,18},{18,26},{... | collective-permute-start | bytes 393224 | tf_op jit(solution)/shard_map/ppermute | solution.py:24
  17.9 24.7 %copy-start.61 = (s32[4]{0:T(128)}, s32[4]{0:T(128)S(1)}, u32[]{:S(2)}) copy-start(s32[4]{0:T(128)S(1)} %fusion.42) | copy-start | bytes 52
  19.2 111.4 %all-to-all-start.1 = ((s32[4,2,1]{1,2,0:T(1,128)}), s32[4,2,1]{1,2,0:T(1,128)}, u32[]{:S(2)}, u32[]{:S(2)}) async-start(s32[4,2,1]{1,2,0:T(1,128)} %bitcast.162), calls=%async_computation.1 | async-start | bytes 4096 | tf_op jit(solution)/shard_map/all_to_all | solution.py:190
  26.3 5.0 %copy-start.57 = (s32[4]{0:T(128)S(1)}, s32[4]{0:T(128)}, u32[]{:S(2)}) copy-start(s32[4]{0:T(128)} %constant.509) | copy-start | bytes 52
  28.8 5.0 %copy-start.56 = (s32[4]{0:T(128)S(1)}, s32[4]{0:T(128)}, u32[]{:S(2)}) copy-start(s32[4]{0:T(128)} %constant.547) | copy-start | bytes 52
  52.4 7.4 %copy-start.55 = (s32[4]{0:T(128)S(1)}, s32[4]{0:T(128)}, u32[]{:S(2)}) copy-start(s32[4]{0:T(128)} %constant.533) | copy-start | bytes 52
  68.1 3.6 %copy-start.38 = (bf16[4,8,8,128]{3,0,2,1:T(4,128)(2,1)S(1)}, bf16[4,8,8,128]{3,0,2,1:T(4,128)(2,1)}, u32[]{:S(2)}) copy-start(bf16[4,8,8,128]{3,0,2,1:T(4,128)(2,1)} %get-tuple-element.42) | copy-start | bytes 196612
  68.1 3.6 %copy-start.39 = (bf16[4,8,8,128]{3,0,2,1:T(4,128)(2,1)S(1)}, bf16[4,8,8,128]{3,0,2,1:T(4,128)(2,1)}, u32[]{:S(2)}) copy-start(bf16[4,8,8,128]{3,0,2,1:T(4,128)(2,1)} %get-tuple-element.43) | copy-start | bytes 196612
  69.1 52.3 %copy-start.24 = (bf16[4,8,8,8,128]{4,3,2,1,0:T(8,128)(2,1)}, bf16[4,8,8,8,128]{4,3,2,1,0:T(8,128)(2,1)S(1)}, u32[]{:S(2)}) copy-start(bf16[4,8,8,8,128]{4,3,2,1,0:T(8,128)(2,1)S(1)} %copy.161) | copy-start | bytes 1572868
  100.5 3.7 %copy-start.44 = (bf16[9,8,128]{2,0,1:T(8,128)(2,1)S(1)}, bf16[9,8,128]{2,0,1:T(8,128)(2,1)}, u32[]{:S(2)}) copy-start(bf16[9,8,128]{2,0,1:T(8,128)(2,1)} %get-tuple-element.142) | copy-start | bytes 55300
  100.6 5.2 %copy-start.54 = (bf16[9,128]{1,0:T(8,128)(2,1)S(1)}, bf16[9,128]{1,0:T(8,128)(2,1)}, u32[]{:S(2)}) copy-start(bf16[9,128]{1,0:T(8,128)(2,1)} %get-tuple-element.148) | copy-start | bytes 6916
  100.6 5.8 %copy-start.53 = (bf16[9,128]{1,0:T(8,128)(2,1)S(1)}, bf16[9,128]{1,0:T(8,128)(2,1)}, u32[]{:S(2)}) copy-start(bf16[9,128]{1,0:T(8,128)(2,1)} %get-tuple-element.146) | copy-start | bytes 6916
  100.6 6.5 %copy-start.52 = (bf16[9,128]{1,0:T(8,128)(2,1)S(1)}, bf16[9,128]{1,0:T(8,128)(2,1)}, u32[]{:S(2)}) copy-start(bf16[9,128]{1,0:T(8,128)(2,1)} %get-tuple-element.149) | copy-start | bytes 6916
  100.6 7.2 %copy-start.51 = (bf16[9,128]{1,0:T(8,128)(2,1)S(1)}, bf16[9,128]{1,0:T(8,128)(2,1)}, u32[]{:S(2)}) copy-start(bf16[9,128]{1,0:T(8,128)(2,1)} %get-tuple-element.147) | copy-start | bytes 6916
  100.6 7.9 %copy-start.41 = (bf16[4,8,128]{2,0,1:T(4,128)(2,1)S(1)}, bf16[4,8,128]{2,0,1:T(4,128)(2,1)}, u32[]{:S(2)}) copy-start(bf16[4,8,128]{2,0,1:T(4,128)(2,1)} %copy-done.40) | copy-start | bytes 24580
  100.6 7.9 %copy-start.43 = (bf16[4,8,128]{2,0,1:T(4,128)(2,1)S(1)}, bf16[4,8,128]{2,0,1:T(4,128)(2,1)}, u32[]{:S(2)}) copy-start(bf16[4,8,128]{2,0,1:T(4,128)(2,1)} %copy-done.42) | copy-start | bytes 24580
  114.6 4.5 %copy-start.5 = (bf16[4,8,8,8,384]{4,3,2,1,0:T(8,128)(2,1)}, bf16[4,8,8,8,384]{4,3,2,1,0:T(8,128)(2,1)S(1)}, u32[]{:S(2)}) copy-start(bf16[4,8,8,8,384]{4,3,2,1,0:T(8,128)(2,1)S(1)} %copy.158) | copy-start | bytes 4718596
  130.6 17.5 %all-to-all-start = ((bf16[8,512,128]{2,1,0:T(8,128)(2,1)}), bf16[8,512,128]{2,1,0:T(8,128)(2,1)S(1)}, u32[]{:S(2)}, u32[]{:S(2)}) async-start(bf16[8,512,128]{2,1,0:T(8,128)(2,1)} %gather_fusion.52), calls=%async_computation | async-start | bytes 2097152 | tf_op jit(solution)/shard_map/all_to_all | solution.py:189
  149.5 5.5 %copy-start.31 = (bf16[1,1,4,512,128]{4,3,2,1,0:T(8,128)(2,1)S(1)}, bf16[1,1,4,512,128]{4,3,2,1,0:T(8,128)(2,1)}, u32[]{:S(2)}) copy-start(bf16[1,1,4,512,128]{4,3,2,1,0:T(8,128)(2,1)} %param.9) | copy-start | bytes 1572868
  149.5 3.1 collective-permute-start.2
  155.9 3.8 %collective-permute-start.3 = (bf16[4,512,128]{2,1,0:T(8,128)(2,1)S(1)}, bf16[4,512,128]{2,1,0:T(8,128)(2,1)S(1)}, u32[]{:S(2)}, u32[]{:S(2)}) collective-permute-start(bf16[4,512,128]{2,1,0:T(8,128)(2,1)S(1)} %bitcast.642), channel_id=1, source_target_pairs={{4,0},{5,1},{6,2},{7,3},{12,8},{13,9},{14,10},{15,11},{20,16},{21,... | collective-permute-start | bytes 1572872 | tf_op jit(solution)/shard_map/ppermute | solution.py:33
  161.4 26.1 %all-to-all-start.2 = ((bf16[8,512,128]{2,1,0:T(8,128)(2,1)}), bf16[8,512,128]{2,1,0:T(8,128)(2,1)}, u32[]{:S(2)}, u32[]{:S(2)}) async-start(bf16[8,512,128]{2,1,0:T(8,128)(2,1)} %gather_fusion.54), calls=%async_computation.2 | async-start | bytes 2097152 | tf_op jit(solution)/shard_map/all_to_all | solution.py:208
  165.7 161.1 %all-reduce.38.cloned.1.call-start = ((), (), s32[]{:S(2)}) async-start(), calls=%async_computation.4 | async-start | bytes 3670016 | tf_op jit(solution)/shard_map/psum | solution.py:219
  185.7 4.5 %copy-start.19 = (f32[2048,128]{1,0:T(8,128)S(1)}, f32[2048,128]{1,0:T(8,128)}, u32[]{:S(2)}) copy-start(f32[2048,128]{1,0:T(8,128)} %copy-done.18) | copy-start | bytes 3145732
  190.2 3.6 %copy-start.16 = (bf16[384,2048]{1,0:T(8,128)(2,1)S(1)}, bf16[384,2048]{1,0:T(8,128)(2,1)}, u32[]{:S(2)}) copy-start(bf16[384,2048]{1,0:T(8,128)(2,1)} %copy.177) | copy-start | bytes 4718596
  203.1 143.0 %all-reduce.36.cloned.1.call-start = ((), (), s32[]{:S(2)}) async-start(), calls=%async_computation.3 | async-start | bytes 131072 | tf_op jit(solution)/shard_map/psum | solution.py:221
  (41 other events, 71.2 us)
Sparse Core Ops, SparseCore 0:
  203.3 123.5 all-reduce.37
  329.2 16.8 all-reduce.35
where the time goes:
time: 358 us; the launch traced here: 356 us
  waiting for transfers between devices  158 us (44%)
  local copies, waits for them, and re-layouts  109 us (30%)
  other arithmetic  37 us (10%)
  starting transfers between devices  22.3 us (6%)
  between operations  15.4 us (4%)
  matrix products  14.4 us (4%)
    psum x1, waiting for transfers between devices, body(): weight_sum = lax.psum(local_taps, ('brick', 'dp'))  124 us
    dot_general x9, local copies, waits for them, and re-layouts, tap_gradients(): lax.dot_general(group_block(padded, move_a, move_b), slope_rows, (((0,),...  20.4 us
    psum x1, waiting for transfers between devices, body(): projection_sum = lax.psum(partial_projection, 'section')  19.3 us
    gather x28, local copies, waits for them, and re-layouts, pad_local(): plane_table[:, source_part[step_b], source_part[step_c]][index_rows]  16.1 us
    unnamed x131, local copies, waits for them, and re-layouts  15.5 us
    gather x18, local copies, waits for them, and re-layouts, pad_local(): far_rows = global_links[chain_rows, 0 if step_a > 0 else 1]  11.3 us
    gather x18, other arithmetic, pad_local(): plane_table[:, source_part[step_b], source_part[step_c]][index_rows]  10.9 us
    all_to_all x1, waiting for transfers between devices, body(): lax.all_to_all(buffer_rows, 'brick', split_axis=0, concat_axis=0, tiled=T...  10.8 us
  transfers between devices with their start and end apart: 9, of which 5 were waited for; matrix products, arithmetic and copies ran while one was open for 36% of the time, Pallas kernels for 0%

commit v1 on v0

v1 whole, which is shorter than its diff:
```python
import functools

import jax
import jax.numpy as jnp
from jax import lax
from jax.experimental import pallas as pl
from jax.experimental.pallas import tpu as pltpu
from jax.sharding import PartitionSpec as P

MESH = pl.DeviceIdType.MESH
f32, bf16 = jnp.float32, jnp.bfloat16
VM = pl.BlockSpec(memory_space=pltpu.VMEM)
SM = pl.BlockSpec(memory_space=pltpu.SMEM)
LIMIT = 56 * 1024 * 1024


def params(collective=None):
    if collective is None:
        return pltpu.CompilerParams(vmem_limit_bytes=LIMIT)
    return pltpu.CompilerParams(
        vmem_limit_bytes=LIMIT, collective_id=collective, has_side_effects=True
    )


def halo_kernel(owners, feats, route, before, after, routes, s_up, r_up, s_dn, r_dn, s_rt, r_rt):
    me = lax.axis_index("brick")
    barrier = pltpu.get_barrier_semaphore()
    for k in range(1, owners):
        pl.semaphore_signal(
            barrier, inc=1, device_id={"brick": lax.rem(me + k, owners)}, device_id_type=MESH
        )
    pl.semaphore_wait(barrier, owners - 1)
    up = pltpu.make_async_remote_copy(
        src_ref=feats.at[:, 7], dst_ref=before, send_sem=s_up, recv_sem=r_up,
        device_id={"brick": lax.rem(me + 1, owners)}, device_id_type=MESH,
    )
    down = pltpu.make_async_remote_copy(
        src_ref=feats.at[:, 0], dst_ref=after, send_sem=s_dn, recv_sem=r_dn,
        device_id={"brick": lax.rem(me + owners - 1, owners)}, device_id_type=MESH,
    )
    up.start()
    down.start()
    sends = []
    for k in range(1, owners):
        copy = pltpu.make_async_remote_copy(
            src_ref=route, dst_ref=routes.at[me], send_sem=s_rt.at[k], recv_sem=r_rt.at[k],
            device_id={"brick": lax.rem(me + k, owners)}, device_id_type=MESH,
        )
        copy.start()
        sends.append(copy)
    routes[me] = route[...]
    for copy in sends:
        copy.wait()
    up.wait()
    down.wait()


def conv_kernel(
    owners, cap, nb, routes, feats, before, after, weights,
    taps, slots, z, tables, full, plus, minus, ext, wide, links,
):
    me = lax.axis_index("brick")
    bricks = feats.shape[0]
    start = me * bricks
    for r in range(bricks):
        up = nb[r, 0]
        dn = nb[r, 1]
        links[r, 0] = jnp.where(up >= 0, up - start, 2 * bricks)
        links[r, 1] = jnp.where(
            dn >= 0, jnp.where(dn >= start, dn - start, dn - start + 2 * bricks), 2 * bricks
        )
        for e in range(2, 6):
            links[r, e] = jnp.where(nb[r, e] >= 0, nb[r, e] - start, bricks)
    for e in range(6):
        links[bricks, e] = jnp.int32(2 * bricks if e < 2 else bricks)
    for i in range(owners * cap):
        tables[2, i] = jnp.int32(0)

    def one_owner(s, carry):
        targets = [lax.div(routes[s, r], bricks) for r in range(bricks)]
        for r in range(bricks):
            count = jnp.int32(0)
            for e in range(r):
                count = count + jnp.where(targets[e] == targets[r], 1, 0)

            @pl.when(s == me)
            def _():
                tables[0, r] = targets[r] * cap + count

            @pl.when(targets[r] == me)
            def _():
                row = lax.rem(routes[s, r], bricks)
                tables[1, row] = s * cap + count
                tables[2, s * cap + count] = row

        return carry

    lax.fori_loop(0, owners, one_owner, 0)

    for p in range(3):
        wide[:, p * 128 : (p + 1) * 128] = weights[9 * p : 9 * p + 9].reshape(1152, 128)
    full[:bricks] = feats[...].astype(f32)
    full[bricks] = jnp.zeros(full.shape[1:], f32)
    plus[:bricks] = feats[:, 0].astype(f32)
    plus[bricks : 2 * bricks] = after[...].astype(f32)
    plus[2 * bricks] = jnp.zeros(plus.shape[1:], f32)
    minus[:bricks] = feats[:, 7].astype(f32)
    minus[bricks : 2 * bricks] = before[...].astype(f32)
    minus[2 * bricks] = jnp.zeros(minus.shape[1:], f32)

    def shifted(t, inside, side):
        if t == 0:
            return inside
        axis = inside.ndim - 2
        place = lax.broadcasted_iota(jnp.int32, inside.shape, axis)
        joined = jnp.where(place == (0 if t > 0 else 7), side, inside)
        return pltpu.roll(joined, 7 if t > 0 else 1, axis)

    def one_brick(r, carry):
        r1 = {0: r, 1: links[r, 4], -1: links[r, 5]}
        r2 = {}
        for t in (-1, 0, 1):
            r2[0, t] = r1[t]
            r2[1, t] = links[r1[t], 2]
            r2[-1, t] = links[r1[t], 3]
        r3 = {}
        for q, t in r2:
            r3[1, q, t] = links[r2[q, t], 0]
            r3[-1, q, t] = links[r2[q, t], 1]
        for t in (-1, 0, 1):
            ext[t + 1, 1:9, 1:9] = shifted(t, full[r], full[r1[t]])
            ext[t + 1, 1:9, 0] = shifted(t, full[r2[-1, 0], :, 7], full[r2[-1, t], :, 7])
            ext[t + 1, 1:9, 9] = shifted(t, full[r2[1, 0], :, 0], full[r2[1, t], :, 0])
            for p, table in ((-1, minus), (1, plus)):
                a = 0 if p < 0 else 9
                ext[t + 1, a, 1:9] = shifted(t, table[r3[p, 0, 0]], table[r3[p, 0, t]])
                ext[t + 1, a, 0] = shifted(t, table[r3[p, -1, 0], 7], table[r3[p, -1, t], 7])
                ext[t + 1, a, 9] = shifted(t, table[r3[p, 1, 0], 0], table[r3[p, 1, t], 0])
        for q in range(3):
            for t in range(3):
                lane = (3 * q + t) * 128
                z[r, :, lane : lane + 128] = (
                    ext[t, :, q : q + 8].reshape(640, 128).astype(bf16)
                )
        product = jnp.dot(z[r], wide[...], preferred_element_type=f32)
        total = product[0:512, 0:128] + product[64:576, 128:256] + product[128:640, 256:384]
        taps[r] = total
        slots[tables[0, r]] = (total / (1.0 + jnp.exp(-total))).astype(bf16)
        return carry

    lax.fori_loop(0, bricks, one_brick, 0)


def skip_kernel(
    owners, cap, tables, taps, slots, projection, cotangent,
    acts, slope, skip, arrived, back, s_sem, r_sem, s_bk, r_bk,
):
    me = lax.axis_index("brick")
    section = lax.axis_index("section")
    bricks = taps.shape[0]
    barrier = pltpu.get_barrier_semaphore()
    for d in range(owners):
        pl.semaphore_signal(
            barrier, inc=1, device_id={"brick": d, "section": 1 - section}, device_id_type=MESH
        )
    pl.semaphore_wait(barrier, owners)

    def move(k, source, sends, receives):
        peer = lax.rem(me + k, owners)
        return pltpu.make_async_remote_copy(
            src_ref=source.at[pl.ds(peer * cap, cap)],
            dst_ref=arrived.at[pl.ds(me * cap, cap)],
            send_sem=sends.at[k], recv_sem=receives.at[k],
            device_id={"brick": peer, "section": 1 - section}, device_id_type=MESH,
        )

    order = [k for k in range(1, owners)] + [0]

    @pl.when(section == 0)
    def _():
        for k in order:
            move(k, slots, s_sem, r_sem).start()
        skip[...] = jnp.zeros(skip.shape, skip.dtype)

        def gate(r, carry):
            v = taps[r]
            acts[r] = (v / (1.0 + jnp.exp(-v))).astype(bf16)
            return carry

        lax.fori_loop(0, bricks, gate, 0)
        for k in order:
            move(k, slots, s_sem, r_sem).wait_send()
        for k in order:
            move(k, back, s_bk, r_bk).wait_recv()

        def last(r, carry):
            v = taps[r]
            g = 1.0 / (1.0 + jnp.exp(-v))
            both = cotangent[r].astype(f32) + arrived[tables[0, r]].astype(f32)
            slope[r] = (both * (g * (1.0 + v * (1.0 - g)))).astype(bf16)
            return carry

        lax.fori_loop(0, bricks, last, 0)

    @pl.when(section == 1)
    def _():
        for k in order:
            move(k, slots, s_sem, r_sem).wait_recv()

        def step(r, carry):
            tile = arrived[tables[1, r]]
            skip[r] = tile
            v = taps[r] + jnp.dot(tile, projection[...], preferred_element_type=f32)
            g = 1.0 / (1.0 + jnp.exp(-v))
            acts[r] = (v * g).astype(bf16)
            slope[r] = (cotangent[r].astype(f32) * (g * (1.0 + v * (1.0 - g)))).astype(bf16)
            return carry

        lax.fori_loop(0, bricks, step, 0)

        def pack(i, carry):
            back[i] = lax.dot_general(
                slope[tables[2, i]], projection[...], (((1,), (1,)), ((), ())),
                preferred_element_type=f32,
            ).astype(bf16)
            return carry

        lax.fori_loop(0, owners * cap, pack, 0)
        for k in order:
            move(k, back, s_bk, r_bk).start()
        for k in order:
            move(k, back, s_bk, r_bk).wait_send()


def grad_kernel(z, slope, skip, out, spread, total):
    bricks = z.shape[0]
    spread[...] = jnp.zeros(spread.shape, bf16)
    total[...] = jnp.zeros(total.shape, f32)

    def one(r, acc):
        for p in range(3):
            spread[p * 64 : p * 64 + 512, p * 128 : (p + 1) * 128] = slope[r]
        total[...] += lax.dot_general(
            z[r], spread[...], (((0,), (0,)), ((), ())), preferred_element_type=f32
        )
        return acc + lax.dot_general(
            skip[r], slope[r], (((0,), (0,)), ((), ())), preferred_element_type=f32
        )

    projected = lax.fori_loop(0, bricks, one, jnp.zeros((128, 128), f32))
    for p in range(3):
        out[1152 * p : 1152 * (p + 1)] = total[:, p * 128 : (p + 1) * 128].astype(bf16)
    out[3456:3584] = projected.astype(bf16)
    if out.shape[0] > 3584:
        out[3584:] = jnp.zeros((out.shape[0] - 3584, 128), bf16)


def sum_kernel(
    owners, scenes, grads, out, proj, rx1, part, rx2, s1, r1, s2, r2, s3, r3, s4, r4, s5, r5
):
    b = lax.axis_index("brick")
    z = lax.axis_index("dp")
    section = lax.axis_index("section")
    rows = grads.shape[0] // (owners * scenes)
    wide = rows * scenes
    barrier = pltpu.get_barrier_semaphore()
    for k in range(1, owners):
        pl.semaphore_signal(
            barrier, inc=1, device_id={"brick": lax.rem(b + k, owners)}, device_id_type=MESH
        )
    for k in range(1, scenes):
        pl.semaphore_signal(
            barrier, inc=1, device_id={"dp": lax.rem(z + k, scenes)}, device_id_type=MESH
        )
    pl.semaphore_signal(barrier, inc=1, device_id={"section": 1 - section}, device_id_type=MESH)
    pl.semaphore_wait(barrier, owners + scenes - 1)

    def chunk(ref, owner, scene):
        return ref.at[pl.ds(pl.multiple_of(owner * wide + scene * rows, 16), rows)]

    started = []

    def send(source, target, s, r, where):
        copy = pltpu.make_async_remote_copy(
            src_ref=source, dst_ref=target, send_sem=s, recv_sem=r,
            device_id=where, device_id_type=MESH,
        )
        copy.start()
        started.append(copy)
        return copy

    along = list(range(1, scenes)) + [0]
    first, second, third, fourth = {}, {}, {}, {}
    for j in along:
        scene = lax.rem(z + j, scenes)
        for k in range(1, owners):
            peer = lax.rem(b + k, owners)
            first[j, k] = send(
                chunk(grads, peer, scene), rx1.at[j, k], s1.at[j, k], r1.at[j, k], {"brick": peer}
            )
    for j in along:
        scene = lax.rem(z + j, scenes)
        for k in range(1, owners):
            first[j, k].wait_recv()
        mine = pl.multiple_of(b * wide + scene * rows, 16)
        summed = grads[pl.ds(mine, rows), :].astype(f32)
        for k in range(1, owners):
            summed = summed + rx1[j, k].astype(f32)
        if j:
            part[j] = summed.astype(bf16)
            second[j] = send(part.at[j], rx2.at[j], s2.at[j], r2.at[j], {"dp": scene})
    for j in range(1, scenes):
        second[j].wait_recv()
        summed = summed + rx2[j].astype(f32)
    mine = pl.multiple_of(b * wide + z * rows, 16)
    out[pl.ds(mine, rows), :] = summed.astype(bf16)
    for j in range(1, scenes):
        third[j] = send(
            chunk(out, b, z), chunk(out, b, z), s3.at[j], r3.at[j],
            {"dp": lax.rem(z + j, scenes)},
        )
    for j in range(scenes):
        scene = lax.rem(z + scenes - j, scenes)
        if j:
            third[j].wait_recv()
        for k in range(1, owners):
            fourth[j, k] = send(
                chunk(out, b, scene), chunk(out, b, scene), s4.at[j, k], r4.at[j, k],
                {"brick": lax.rem(b + k, owners)},
            )
    for copy in fourth.values():
        copy.wait_recv()
    last = pltpu.make_async_remote_copy(
        src_ref=out.at[pl.ds(3456, 128)], dst_ref=proj, send_sem=s5, recv_sem=r5,
        device_id={"section": 1 - section}, device_id_type=MESH,
    )

    @pl.when(section == 1)
    def _():
        last.start()
        proj[...] = out[3456:3584, :]
        last.wait_send()

    @pl.when(section == 0)
    def _():
        last.wait_recv()

    for copy in started:
        copy.wait_send()


def body(features, weights, projection, cotangent, neighbours, route):
    bricks, channels = features.shape[2], features.shape[-1]
    owners, scenes = lax.axis_size("brick"), lax.axis_size("dp")
    cap = max(2, 3 * bricks // (2 * owners))
    feats = features[0, 0].reshape(bricks, 8, 8, 8, channels)
    dma, arr = pltpu.SemaphoreType.DMA, jax.ShapeDtypeStruct
    route_tile = jnp.pad(route, ((0, 7), (0, 128 - bricks)))
    plane = (bricks, 8, 8, channels)
    before, after, routes = pl.pallas_call(
        functools.partial(halo_kernel, owners),
        out_shape=[arr(plane, bf16), arr(plane, bf16), arr((owners, 8, 128), jnp.int32)],
        in_specs=[VM, VM],
        out_specs=[VM, VM, VM],
        scratch_shapes=[dma, dma, dma, dma, dma((owners,)), dma((owners,))],
        compiler_params=params(0),
    )(feats, route_tile)

    count = owners * cap
    taps, slots, z, tables = pl.pallas_call(
        functools.partial(conv_kernel, owners, cap),
        out_shape=[
            arr((bricks, 512, channels), f32),
            arr((count, 512, channels), bf16),
            arr((bricks, 640, 9 * channels), bf16),
            arr((3, max(count, bricks)), jnp.int32),
        ],
        in_specs=[SM, SM, VM, VM, VM, VM],
        out_specs=[VM, VM, VM, SM],
        scratch_shapes=[
            pltpu.VMEM((bricks + 1, 8, 8, 8, channels), f32),
            pltpu.VMEM((2 * bricks + 1, 8, 8, channels), f32),
            pltpu.VMEM((2 * bricks + 1, 8, 8, channels), f32),
            pltpu.VMEM((3, 10, 10, 8, channels), f32),
            pltpu.VMEM((9 * channels, 3 * channels), bf16),
            pltpu.SMEM((bricks + 1, 6), jnp.int32),
        ],
        compiler_params=params(),
    )(neighbours[0, 0], routes[:, 0, :bricks], feats, before, after, weights[0])

    tile = (bricks, 512, channels)
    acts, slope, skip = pl.pallas_call(
        functools.partial(skip_kernel, owners, cap),
        out_shape=[arr(tile, bf16)] * 3,
        in_specs=[SM, VM, VM, VM, VM],
        out_specs=[VM, VM, VM],
        scratch_shapes=[
            pltpu.VMEM((count, 512, channels), bf16),
            pltpu.VMEM((count, 512, channels), bf16),
            dma((owners,)), dma((owners,)), dma((owners,)), dma((owners,)),
        ],
        compiler_params=params(1),
    )(tables, taps, slots, projection, cotangent[0, 0])

    unit = 16 * owners * scenes
    total = -(-28 * channels // unit) * unit
    grads = pl.pallas_call(
        grad_kernel,
        out_shape=arr((total, channels), bf16),
        in_specs=[VM, VM, VM],
        out_specs=VM,
        scratch_shapes=[
            pltpu.VMEM((640, 3 * channels), bf16),
            pltpu.VMEM((9 * channels, 3 * channels), f32),
        ],
        compiler_params=params(),
    )(z, slope, skip)

    rows = total // (owners * scenes)
    summed, projected = pl.pallas_call(
        functools.partial(sum_kernel, owners, scenes),
        out_shape=[arr((total, channels), bf16), arr((channels, channels), bf16)],
        in_specs=[VM],
        out_specs=[VM, VM],
        scratch_shapes=[
            pltpu.VMEM((scenes, owners, rows, channels), bf16),
            pltpu.VMEM((scenes, rows, channels), bf16),
            pltpu.VMEM((scenes, rows, channels), bf16),
            dma((scenes, owners)), dma((scenes, owners)),
            dma((scenes,)), dma((scenes,)),
            dma((scenes,)), dma((scenes,)),
            dma((scenes, owners)), dma((scenes, owners)),
            dma, dma,
        ],
        compiler_params=params(2),
    )(grads)
    return (
        acts[None, None],
        summed[: 27 * channels].astype(f32).reshape(1, 27, channels, channels),
        projected.astype(f32),
    )


def solution(mesh):
    return jax.shard_map(
        body,
        mesh=mesh,
        in_specs=(
            P("section", "dp", "brick", None, None),
            P("section", None, None, None),
            P(),
            P("section", "dp", "brick", None, None),
            P("section", "dp", "brick", None),
            P("dp", "brick"),
        ),
        out_specs=(P("section", "dp", "brick", None, None), P("section", None, None, None), P()),
        check_vma=False,
    )
```

time: 358 us -> 89.4 us (0.25)
  waiting for transfers between devices: 158 us -> 0 us
  local copies, waits for them, and re-layouts: 109 us -> 4.57 us
  Pallas kernels: 0 us -> 81 us
  other arithmetic: 37 us -> 2.8 us
  starting transfers between devices: 22.3 us -> 0 us
  between operations: 15.4 us -> 0.68 us
  matrix products: 14.4 us -> 0 us
    psum x2 -> x0, waiting for transfers between devices: 143 us -> none  [the longest x1 124 us: body(): weight_sum = lax.psum(local_taps, ('brick', 'dp'))]
    pallas_call x0 -> x5, Pallas kernels: none -> 81 us  [the longest x1 30.9 us: body(): pl.pallas_call(functools.partial(sum_kernel, owners, scenes), out_shape=[...]
    gather x74 -> x0, local copies, waits for them, and re-layouts: 44.7 us -> none  [the longest x28 16.1 us: pad_local(): plane_table[:, source_part[step_b], source_part[step_c]][index_rows]]
    dot_general x9 -> x0, local copies, waits for them, and re-layouts: 20.4 us -> none  [tap_gradients(): lax.dot_general(group_block(padded, move_a, move_b), slope_rows, (((0,),...]
    concatenate x21 -> x0, other arithmetic: 19.1 us -> none  [the longest x8 9.11 us: group_block(): joined = jnp.concatenate(parts, -1)]
    unnamed x131 -> x3, local copies, waits for them, and re-layouts: 15.5 us -> 0.8 us
    dot_general x21 -> x0, matrix products: 14.4 us -> none  [the longest x9 6.19 us: apply_taps(): jnp.dot(group_block(padded, move_a, move_b), stacked_weights, preferred_e...]
    slice x21 -> x2, local copies, waits for them, and re-layouts: 15.2 us -> 2.52 us  [the longest x1 1.3 us: body(): routes[:, 0, :bricks]]
  transfers between devices with their start and end apart: 9 -> 0, of which waited for: 5 -> 0; matrix products, arithmetic and copies ran while one was open for 36% -> 0% of each run, Pallas kernels for 0% -> 0%
where the time goes in v1:
time: 89.4 us; the launch traced here: 89 us
  Pallas kernels  81 us (91%)
  local copies, waits for them, and re-layouts  4.57 us (5%)
  other arithmetic  2.8 us (3%)
    pallas_call x1, Pallas kernels, body(): pl.pallas_call(functools.partial(sum_kernel, owners, scenes), out_shape=[...  30.9 us
    pallas_call x1, Pallas kernels, body(): pl.pallas_call(functools.partial(skip_kernel, owners, cap), out_shape=[ar...  22.6 us
    pallas_call x1, Pallas kernels, body(): pl.pallas_call(functools.partial(halo_kernel, owners), out_shape=[arr(pla...  9.67 us
    pallas_call x1, Pallas kernels, body(): pl.pallas_call(functools.partial(conv_kernel, owners, cap), out_shape=[ar...  9.16 us
    pallas_call x1, Pallas kernels, body(): pl.pallas_call(grad_kernel, out_shape=arr((total, channels), bf16), in_sp...  8.59 us

profile of v1, /device:TPU:0, one launch (start us, length us, event | category | flops | bytes accessed | tf_op | source)
XLA Modules:
  0.0 89.0 jit_solution(11675813428978806916)
XLA Ops:
  0.6 1.3 %pad.4.route = s32[8,128]{1,0:T(8,128)} pad(s32[1,4]{1,0:T(1,128)} %param.11, s32[]{:T(128)} %constant.0.clone.1), padding=0_7x0_124 | pad | bytes 4116 | tf_op jit(solution)/shard_map/jit(_pad)/pad | solution.py:358
  1.9 9.7 %shard_map.85 = (bf16[4,8,8,128]{3,2,1,0:T(8,128)(2,1)}, bf16[4,8,8,128]{3,2,1,0:T(8,128)(2,1)}, s32[4,8,128]{2,1,0:T(8,128)}) custom-call(bf16[4,8,8,8,128]{4,3,2,1,0:T(8,128)(2,1)} %bitcast.9, s32[8,128]{1,0:T(8,128)} %pad.4.route), custom_call_target="tpu_custom_call" | custom-call | tf_op jit(solution)/shard_map/pallas_call | solution.py:360
  11.6 1.3 %slice.6 = s32[4,1,4]{2,1,0:T(1,128)} slice(s32[4,8,128]{2,1,0:T(8,128)} %get-tuple-element.15), slice={[0:4], [0:1], [0:4]} | slice | bytes 128 | tf_op jit(solution)/shard_map/slice | solution.py:389
  12.9 9.2 %shard_map.86 = (f32[4,512,128]{2,1,0:T(8,128)}, bf16[8,512,128]{2,1,0:T(8,128)(2,1)}, bf16[4,640,1152]{2,1,0:T(8,128)(2,1)}, s32[3,8]{1,0:T(4,128)}) custom-call(s32[4,6]{1,0:T(4,128)} %bitcast.15, s32[4,4]{1,0:T(4,128)} %bitcast.14, bf16[4,8,8,8,128]{4,3,2,1,0:T(8,128)(2,1)} %bitcast.10, bf16[4,8,8,128]{3,2,1,0:T(8,128)(2,1)} %get-tuple-element.16.before, ...), custom_call_target="tpu_custom_call" | custom-call | tf_op jit(solution)/shard_map/pallas_call | solution.py:370
  22.0 22.6 %shard_map.87 = (bf16[4,512,128]{2,1,0:T(8,128)(2,1)}, bf16[4,512,128]{2,1,0:T(8,128)(2,1)}, bf16[4,512,128]{2,1,0:T(8,128)(2,1)}) custom-call(s32[3,8]{1,0:T(4,128)} %get-tuple-element.18.tables, f32[4,512,128]{2,1,0:T(8,128)} %get-tuple-element.19.taps, bf16[8,512,128]{2,1,0:T(8,128)(2,1)} %get-tuple-element.20.slots, bf16[128,128]{1,0:T(8,128)(2,1)} %projection.1, ...), custom_call_target="tpu_custom_call" | custom-call | tf_op jit(solution)/shard_map/pallas_call | solution.py:392
  44.6 0.0 copy-start
  44.7 8.6 %shard_map.88.grads = bf16[3584,128]{1,0:T(8,128)(2,1)} custom-call(bf16[4,640,1152]{2,1,0:T(8,128)(2,1)} %get-tuple-element.22.z, bf16[4,512,128]{2,1,0:T(8,128)(2,1)} %get-tuple-element.23.slope, bf16[4,512,128]{2,1,0:T(8,128)(2,1)} %get-tuple-element.24.skip), custom_call_target="tpu_custom_call" | custom-call | tf_op jit(solution)/shard_map/pallas_call | solution.py:407
  53.2 30.9 %shard_map.89 = (bf16[3584,128]{1,0:T(8,128)(2,1)}, bf16[128,128]{1,0:T(8,128)(2,1)}) custom-call(bf16[3584,128]{1,0:T(8,128)(2,1)} %shard_map.88.grads), custom_call_target="tpu_custom_call" | custom-call | tf_op jit(solution)/shard_map/pallas_call | solution.py:420
  84.2 1.2 %slice.7 = bf16[3456,128]{1,0:T(8,128)(2,1)S(1)} slice(bf16[3584,128]{1,0:T(8,128)(2,1)} %get-tuple-element.25), slice={[0:3456], [0:128]} | slice | bytes 1769472 | tf_op jit(solution)/shard_map/slice | solution.py:439
  85.4 1.4 %convert_element_type.4 = f32[128,128]{1,0:T(8,128)} convert(bf16[128,128]{1,0:T(8,128)(2,1)} %get-tuple-element.26) | non-fusion elementwise | flops 16384 | bytes 98304 | tf_op jit(solution)/shard_map/convert_element_type | solution.py:440
  86.8 1.4 %convert.1 = f32[1,27,128,128]{3,2,1,0:T(8,128)} convert(bf16[1,27,128,128]{3,2,1,0:T(8,128)(2,1)S(1)} %bitcast.8) | non-fusion elementwise | flops 442368 | bytes 2654208 | tf_op jit(solution)/shard_map/reshape | solution.py:439
  88.2 0.0 copy-done
  88.2 0.8 copy.10
Async XLA Ops:
  44.6 43.6 %copy-start = (bf16[4,512,128]{2,1,0:T(8,128)(2,1)S(1)}, bf16[4,512,128]{2,1,0:T(8,128)(2,1)}, u32[]{:S(2)}) copy-start(bf16[4,512,128]{2,1,0:T(8,128)(2,1)} %get-tuple-element.21) | copy-start | bytes 1572868

commit v2 on v1

v2 whole, which is shorter than its diff:
```python
import functools

import jax
import jax.numpy as jnp
from jax import lax
from jax.experimental import pallas as pl
from jax.experimental.pallas import tpu as pltpu
from jax.sharding import PartitionSpec as P

MESH = pl.DeviceIdType.MESH
f32, bf16 = jnp.float32, jnp.bfloat16
VM = pl.BlockSpec(memory_space=pltpu.VMEM)
SM = pl.BlockSpec(memory_space=pltpu.SMEM)
LIMIT = 56 * 1024 * 1024


def params(collective=None):
    if collective is None:
        return pltpu.CompilerParams(vmem_limit_bytes=LIMIT)
    return pltpu.CompilerParams(
        vmem_limit_bytes=LIMIT, collective_id=collective, has_side_effects=True
    )


def halo_kernel(owners, feats, route, before, after, routes, s_up, r_up, s_dn, r_dn, s_rt, r_rt):
    me = lax.axis_index("brick")
    barrier = pltpu.get_barrier_semaphore()
    for k in range(1, owners):
        pl.semaphore_signal(
            barrier, inc=1, device_id={"brick": lax.rem(me + k, owners)}, device_id_type=MESH
        )
    pl.semaphore_wait(barrier, owners - 1)
    up = pltpu.make_async_remote_copy(
        src_ref=feats.at[:, 7], dst_ref=before, send_sem=s_up, recv_sem=r_up,
        device_id={"brick": lax.rem(me + 1, owners)}, device_id_type=MESH,
    )
    down = pltpu.make_async_remote_copy(
        src_ref=feats.at[:, 0], dst_ref=after, send_sem=s_dn, recv_sem=r_dn,
        device_id={"brick": lax.rem(me + owners - 1, owners)}, device_id_type=MESH,
    )
    up.start()
    down.start()
    sends = []
    for k in range(1, owners):
        copy = pltpu.make_async_remote_copy(
            src_ref=route, dst_ref=routes.at[me], send_sem=s_rt.at[k], recv_sem=r_rt.at[k],
            device_id={"brick": lax.rem(me + k, owners)}, device_id_type=MESH,
        )
        copy.start()
        sends.append(copy)
    routes[me] = route[...]
    for copy in sends:
        copy.wait()
    up.wait()
    down.wait()


def conv_kernel(
    owners, cap, nb, routes, feats, before, after, weights,
    taps, slots, z, tables, full, plus, minus, ext, wide, links,
):
    me = lax.axis_index("brick")
    bricks = feats.shape[0]
    start = me * bricks
    for r in range(bricks):
        up = nb[r, 0]
        dn = nb[r, 1]
        links[r, 0] = jnp.where(up >= 0, up - start, 2 * bricks)
        links[r, 1] = jnp.where(
            dn >= 0, jnp.where(dn >= start, dn - start, dn - start + 2 * bricks), 2 * bricks
        )
        for e in range(2, 6):
            links[r, e] = jnp.where(nb[r, e] >= 0, nb[r, e] - start, bricks)
    for e in range(6):
        links[bricks, e] = jnp.int32(2 * bricks if e < 2 else bricks)
    for i in range(owners * cap):
        tables[2, i] = jnp.int32(0)

    def one_owner(s, carry):
        targets = [lax.div(routes[s, 0, r], bricks) for r in range(bricks)]
        for r in range(bricks):
            count = jnp.int32(0)
            for e in range(r):
                count = count + jnp.where(targets[e] == targets[r], 1, 0)

            @pl.when(s == me)
            def _():
                tables[0, r] = targets[r] * cap + count

            @pl.when(targets[r] == me)
            def _():
                row = lax.rem(routes[s, 0, r], bricks)
                tables[1, row] = s * cap + count
                tables[2, s * cap + count] = row

        return carry

    lax.fori_loop(0, owners, one_owner, 0)

    for p in range(3):
        wide[:, p * 128 : (p + 1) * 128] = weights[9 * p : 9 * p + 9].reshape(1152, 128)
    full[:bricks] = feats[...].astype(f32)
    full[bricks] = jnp.zeros(full.shape[1:], f32)
    plus[:bricks] = feats[:, 0].astype(f32)
    plus[bricks : 2 * bricks] = after[...].astype(f32)
    plus[2 * bricks] = jnp.zeros(plus.shape[1:], f32)
    minus[:bricks] = feats[:, 7].astype(f32)
    minus[bricks : 2 * bricks] = before[...].astype(f32)
    minus[2 * bricks] = jnp.zeros(minus.shape[1:], f32)

    def shifted(t, inside, side):
        if t == 0:
            return inside
        axis = inside.ndim - 2
        place = lax.broadcasted_iota(jnp.int32, inside.shape, axis)
        joined = jnp.where(place == (0 if t > 0 else 7), side, inside)
        return pltpu.roll(joined, 7 if t > 0 else 1, axis)

    def one_brick(r, carry):
        r1 = {0: r, 1: links[r, 4], -1: links[r, 5]}
        r2 = {}
        for t in (-1, 0, 1):
            r2[0, t] = r1[t]
            r2[1, t] = links[r1[t], 2]
            r2[-1, t] = links[r1[t], 3]
        r3 = {}
        for q, t in r2:
            r3[1, q, t] = links[r2[q, t], 0]
            r3[-1, q, t] = links[r2[q, t], 1]
        for t in (-1, 0, 1):
            ext[t + 1, 1:9, 1:9] = shifted(t, full[r], full[r1[t]])
            ext[t + 1, 1:9, 0] = shifted(t, full[r2[-1, 0], :, 7], full[r2[-1, t], :, 7])
            ext[t + 1, 1:9, 9] = shifted(t, full[r2[1, 0], :, 0], full[r2[1, t], :, 0])
            for p, table in ((-1, minus), (1, plus)):
                a = 0 if p < 0 else 9
                ext[t + 1, a, 1:9] = shifted(t, table[r3[p, 0, 0]], table[r3[p, 0, t]])
                ext[t + 1, a, 0] = shifted(t, table[r3[p, -1, 0], 7], table[r3[p, -1, t], 7])
                ext[t + 1, a, 9] = shifted(t, table[r3[p, 1, 0], 0], table[r3[p, 1, t], 0])
        for q in range(3):
            for t in range(3):
                lane = (3 * q + t) * 128
                z[r, :, lane : lane + 128] = (
                    ext[t, :, q : q + 8].reshape(640, 128).astype(bf16)
                )
        product = jnp.dot(z[r], wide[...], preferred_element_type=f32)
        total = product[0:512, 0:128] + product[64:576, 128:256] + product[128:640, 256:384]
        taps[r] = total
        slots[tables[0, r]] = (total / (1.0 + jnp.exp(-total))).astype(bf16)
        return carry

    lax.fori_loop(0, bricks, one_brick, 0)


def reduce_part(grads, out, base, outer, inner, rx1, part, rx2, sems, started):
    (outer_name, n1), (inner_name, n2) = outer, inner
    x, y = lax.axis_index(outer_name), lax.axis_index(inner_name)
    rows = rx2.shape[1]
    s1, r1, s2, r2, s3, r3, s4, r4 = sems

    def chunk(ref, i, j):
        return ref.at[pl.ds(pl.multiple_of(base + (i * n2 + j) * rows, 16), rows)]

    def load(ref, i, j):
        return ref[pl.ds(pl.multiple_of(base + (i * n2 + j) * rows, 16), rows), :]

    def send(source, target, s, r, where):
        copy = pltpu.make_async_remote_copy(
            src_ref=source, dst_ref=target, send_sem=s, recv_sem=r,
            device_id=where, device_id_type=MESH,
        )
        copy.start()
        started.append(copy)
        return copy

    def other(k):
        return lax.rem(x + k, n1)

    def along(j):
        return lax.rem(y + j, n2)

    order = list(range(1, n2)) + [0]
    first, second, third, fourth = {}, {}, {}, {}
    held = []

    def scatter():
        for j in order:
            for k in range(1, n1):
                first[j, k] = send(
                    chunk(grads, other(k), along(j)), rx1.at[j, k], s1.at[j, k], r1.at[j, k],
                    {outer_name: other(k)},
                )

    def forward(j):
        for k in range(1, n1):
            first[j, k].wait_recv()
        summed = load(grads, x, along(j)).astype(f32)
        for k in range(1, n1):
            summed = summed + rx1[j, k].astype(f32)
        part[j] = summed.astype(bf16) if j else jnp.zeros(part.shape[1:], bf16)
        if j:
            second[j] = send(
                part.at[j], rx2.at[j], s2.at[j], r2.at[j], {inner_name: along(j)}
            )
        else:
            held.append(summed)

    def spread_out(j, scene):
        for k in range(1, n1):
            fourth[j, k] = send(
                chunk(out, x, scene), chunk(out, x, scene), s4.at[j, k], r4.at[j, k],
                {outer_name: other(k)},
            )

    def finish():
        summed = held[0]
        for j in range(1, n2):
            second[j].wait_recv()
            summed = summed + rx2[j].astype(f32)
        out[pl.ds(pl.multiple_of(base + (x * n2 + y) * rows, 16), rows), :] = summed.astype(bf16)
        for j in range(1, n2):
            third[j] = send(
                chunk(out, x, y), chunk(out, x, y), s3.at[j], r3.at[j], {inner_name: along(j)}
            )
        spread_out(0, y)

    def gather(j):
        third[j].wait_recv()
        spread_out(j, lax.rem(y + n2 - j, n2))

    def end():
        for copy in fourth.values():
            copy.wait_recv()

    return scatter, forward, finish, gather, end, order


def back_kernel(
    owners, scenes, cap, split, tables, taps, slots, projection, cotangent, z_far,
    acts, out, proj,
    z, slope, skip, factor, lifted, arrived, back, spread, total, grads, rx, part,
    rx2a, rx2b, rx1b, partb, z_sem, s_sem, r_sem, s_bk, r_bk, *rest,
):
    me = lax.axis_index("brick")
    scene = lax.axis_index("dp")
    section = lax.axis_index("section")
    bricks = taps.shape[0]
    z_copy = pltpu.make_async_copy(z_far, z, z_sem)
    z_copy.start()
    barrier = pltpu.get_barrier_semaphore()
    for d in range(owners):
        pl.semaphore_signal(
            barrier, inc=1, device_id={"brick": d, "section": 1 - section}, device_id_type=MESH
        )
    for k in range(1, owners):
        pl.semaphore_signal(
            barrier, inc=1, device_id={"brick": lax.rem(me + k, owners)}, device_id_type=MESH
        )
    for k in range(1, scenes):
        pl.semaphore_signal(
            barrier, inc=1, device_id={"dp": lax.rem(scene + k, scenes)}, device_id_type=MESH
        )
    pl.semaphore_wait(barrier, 2 * owners - 1 + scenes - 1)

    pieces = s_sem.shape[0]
    height = 512 // pieces

    def move(c, k, source, sends, receives):
        peer = lax.rem(me + k, owners)
        return pltpu.make_async_remote_copy(
            src_ref=source.at[pl.ds(peer * cap, cap), pl.ds(c * height, height)],
            dst_ref=arrived[c].at[pl.ds(me * cap, cap)],
            send_sem=sends.at[c, k], recv_sem=receives.at[c, k],
            device_id={"brick": peer, "section": 1 - section}, device_id_type=MESH,
        )

    order = [k for k in range(1, owners)] + [0]

    @pl.when(section == 0)
    def _():
        for c in range(pieces):
            for k in order:
                move(c, k, slots, s_sem, r_sem).start()
        skip[...] = jnp.zeros(skip.shape, skip.dtype)

        def gate(r, carry):
            v = taps[r]
            g = 1.0 / (1.0 + jnp.exp(-v))
            acts[r] = (v * g).astype(bf16)
            factor[r] = g * (1.0 + v * (1.0 - g))
            return carry

        lax.fori_loop(0, bricks, gate, 0)
        for c in range(pieces):
            for k in order:
                move(c, k, back, s_bk, r_bk).wait_recv()
            span = slice(c * height, (c + 1) * height)

            def last(r, carry):
                both = cotangent[r, span].astype(f32) + arrived[c][tables[0, r]].astype(f32)
                slope[r, span] = (both * factor[r, span]).astype(bf16)
                return carry

            lax.fori_loop(0, bricks, last, 0)

    @pl.when(section == 1)
    def _():
        for c in range(pieces):
            for k in order:
                move(c, k, slots, s_sem, r_sem).wait_recv()
            span = slice(c * height, (c + 1) * height)

            def step(r, carry):
                tile = arrived[c][tables[1, r]]
                skip[r, span] = tile
                v = taps[r, span] + jnp.dot(tile, projection[...], preferred_element_type=f32)
                g = 1.0 / (1.0 + jnp.exp(-v))
                acts[r, span] = (v * g).astype(bf16)
                down = (cotangent[r, span].astype(f32) * (g * (1.0 + v * (1.0 - g)))).astype(bf16)
                slope[r, span] = down
                lifted[r, span] = lax.dot_general(
                    down, projection[...], (((1,), (1,)), ((), ())), preferred_element_type=f32
                ).astype(bf16)
                return carry

            lax.fori_loop(0, bricks, step, 0)

            def pack(i, carry):
                back[i, span] = lifted[tables[2, i], span]
                return carry

            lax.fori_loop(0, owners * cap, pack, 0)
            for k in order:
                move(c, k, back, s_bk, r_bk).start()

    z_copy.wait()
    spread[...] = jnp.zeros(spread.shape, bf16)
    total[...] = jnp.zeros(total.shape, f32)

    def one(r, acc):
        for p in range(3):
            spread[p * 64 : p * 64 + 512, p * 128 : (p + 1) * 128] = slope[r]
        total[...] += lax.dot_general(
            z[r], spread[...], (((0,), (0,)), ((), ())), preferred_element_type=f32
        )
        return acc + lax.dot_general(
            skip[r], slope[r], (((0,), (0,)), ((), ())), preferred_element_type=f32
        )

    projected = lax.fori_loop(0, bricks, one, jnp.zeros((128, 128), f32))
    for p in range(3):
        grads[1152 * p : 1152 * (p + 1)] = total[:, p * 128 : (p + 1) * 128].astype(bf16)
    grads[3456:3584] = projected.astype(bf16)
    if grads.shape[0] > 3584:
        grads[3584:] = jnp.zeros((grads.shape[0] - 3584, 128), bf16)

    started = []
    on_brick, on_dp = ("brick", owners), ("dp", scenes)
    one_part = reduce_part(grads, out, 0, on_brick, on_dp, rx, part, rx2a, rest[:8], started)
    two_part = reduce_part(
        grads, out, split, on_dp, on_brick, rx1b, partb, rx2b, rest[8:16], started
    )
    both = (one_part, two_part)
    for way in both:
        way[0]()
    for i in range(max(owners, scenes)):
        for way in both:
            if i < len(way[5]):
                way[1](way[5][i])
    for way in both:
        way[2]()
    for i in range(1, max(owners, scenes)):
        for way in both:
            if i < len(way[5]):
                way[3](i)
    for way in both:
        way[4]()
    s5, r5 = rest[16:18]
    last_copy = pltpu.make_async_remote_copy(
        src_ref=out.at[pl.ds(3456, 128)], dst_ref=proj, send_sem=s5, recv_sem=r5,
        device_id={"section": 1 - section}, device_id_type=MESH,
    )

    @pl.when(section == 1)
    def _():
        last_copy.start()
        proj[...] = out[3456:3584, :]
        last_copy.wait_send()
        for c in range(pieces):
            for k in order:
                move(c, k, back, s_bk, r_bk).wait_send()

    @pl.when(section == 0)
    def _():
        last_copy.wait_recv()
        for c in range(pieces):
            for k in order:
                move(c, k, slots, s_sem, r_sem).wait_send()

    for copy in started:
        copy.wait_send()


def tail_kernel(summed, projected, acts, weight_out, proj_out, acts_out):
    weight_out[...] = summed[...].astype(f32)
    proj_out[...] = projected[...].astype(f32)
    acts_out[...] = acts[...]


def body(features, weights, projection, cotangent, neighbours, route):
    bricks, channels = features.shape[2], features.shape[-1]
    owners, scenes = lax.axis_size("brick"), lax.axis_size("dp")
    cap = max(2, 3 * bricks // (2 * owners))
    feats = features[0, 0].reshape(bricks, 8, 8, 8, channels)
    dma, arr = pltpu.SemaphoreType.DMA, jax.ShapeDtypeStruct
    plane = (bricks, 8, 8, channels)
    before, after, routes = pl.pallas_call(
        functools.partial(halo_kernel, owners),
        out_shape=[arr(plane, bf16), arr(plane, bf16), arr((owners, 1, bricks), jnp.int32)],
        in_specs=[VM, VM],
        out_specs=[VM, VM, VM],
        scratch_shapes=[dma, dma, dma, dma, dma((owners,)), dma((owners,))],
        compiler_params=params(0),
    )(feats, route)

    count = owners * cap
    taps, slots, z, tables = pl.pallas_call(
        functools.partial(conv_kernel, owners, cap),
        out_shape=[
            arr((bricks, 512, channels), f32),
            arr((count, 512, channels), bf16),
            arr((bricks, 640, 9 * channels), bf16),
            arr((3, max(count, bricks)), jnp.int32),
        ],
        in_specs=[SM, SM, VM, VM, VM, VM],
        out_specs=[VM, VM, VM, SM],
        scratch_shapes=[
            pltpu.VMEM((bricks + 1, 8, 8, 8, channels), f32),
            pltpu.VMEM((2 * bricks + 1, 8, 8, channels), f32),
            pltpu.VMEM((2 * bricks + 1, 8, 8, channels), f32),
            pltpu.VMEM((3, 10, 10, 8, channels), f32),
            pltpu.VMEM((9 * channels, 3 * channels), bf16),
            pltpu.SMEM((bricks + 1, 6), jnp.int32),
        ],
        compiler_params=params(),
    )(neighbours[0, 0], routes, feats, before, after, weights[0])

    tile = (bricks, 512, channels)
    unit = 16 * owners * scenes
    units = -(-28 * channels // unit)
    total = units * unit
    split = (2 * units + 2) // 3 * unit
    height_a, height_b = split // (owners * scenes), (total - split) // (owners * scenes)
    pieces = 4
    vm = pltpu.VMEM
    acts, summed, projected = pl.pallas_call(
        functools.partial(back_kernel, owners, scenes, cap, split),
        out_shape=[
            arr(tile, bf16), arr((total, channels), bf16), arr((channels, channels), bf16)
        ],
        in_specs=[SM, VM, VM, VM, VM, pl.BlockSpec(memory_space=pl.ANY)],
        out_specs=[VM, VM, VM],
        scratch_shapes=[
            vm(z.shape, bf16), vm(tile, bf16), vm(tile, bf16), vm(tile, f32), vm(tile, bf16),
            [vm((count, 512 // pieces, channels), bf16) for _ in range(pieces)],
            vm((count, 512, channels), bf16),
            vm((640, 3 * channels), bf16), vm((9 * channels, 3 * channels), f32),
            vm((total, channels), bf16),
            vm((scenes, owners, height_a, channels), bf16),
            vm((scenes, height_a, channels), bf16),
            vm((scenes, height_a, channels), bf16),
            vm((owners, height_b, channels), bf16),
            vm((owners, scenes, height_b, channels), bf16),
            vm((owners, height_b, channels), bf16),
            dma,
            *[dma((pieces, owners)) for _ in range(4)],
            dma((scenes, owners)), dma((scenes, owners)),
            *[dma((scenes,)) for _ in range(4)],
            dma((scenes, owners)), dma((scenes, owners)),
            dma((owners, scenes)), dma((owners, scenes)),
            *[dma((owners,)) for _ in range(4)],
            dma((owners, scenes)), dma((owners, scenes)),
            dma, dma,
        ],
        compiler_params=params(1),
    )(tables, taps, slots, projection, cotangent[0, 0], z)

    piece = 27 * channels // bricks
    weight_sum, projection_sum, acts = pl.pallas_call(
        tail_kernel,
        grid=(bricks,),
        out_shape=[
            arr((27 * channels, channels), f32), arr((channels, channels), f32), arr(tile, bf16)
        ],
        in_specs=[
            pl.BlockSpec((piece, channels), lambda i: (i, 0)),
            pl.BlockSpec((channels, channels), lambda i: (0, 0)),
            pl.BlockSpec((1, 512, channels), lambda i: (i, 0, 0)),
        ],
        out_specs=[
            pl.BlockSpec((piece, channels), lambda i: (i, 0)),
            pl.BlockSpec((channels, channels), lambda i: (0, 0)),
            pl.BlockSpec((1, 512, channels), lambda i: (i, 0, 0)),
        ],
        compiler_params=params(),
    )(summed, projected, acts)
    return (
        acts[None, None],
        weight_sum.reshape(1, 27, channels, channels),
        projection_sum,
    )


def solution(mesh):
    return jax.shard_map(
        body,
        mesh=mesh,
        in_specs=(
            P("section", "dp", "brick", None, None),
            P("section", None, None, None),
            P(),
            P("section", "dp", "brick", None, None),
            P("section", "dp", "brick", None),
            P("dp", "brick"),
        ),
        out_specs=(P("section", "dp", "brick", None, None), P("section", None, None, None), P()),
        check_vma=False,
    )
```

time: 89.4 us -> 72.2 us (0.81)
  Pallas kernels: 81 us -> 71.3 us
  local copies, waits for them, and re-layouts: 4.57 us -> 0 us
  other arithmetic: 2.8 us -> 0 us
    pallas_call x3 -> x2, Pallas kernels: 62.1 us -> 52.6 us  [the longest x1 48.8 us: body(): pl.pallas_call(functools.partial(back_kernel, owners, scenes, cap, split)...]
    slice x2 -> x0, local copies, waits for them, and re-layouts: 2.52 us -> none  [the longest x1 1.3 us: body(): routes[:, 0, :bricks]]
    reshape x1 -> x0, other arithmetic: 1.41 us -> none  [body(): summed[:27 * channels].astype(f32).reshape(1, 27, channels, channels)]
    convert_element_type x1 -> x0, other arithmetic: 1.39 us -> none  [body(): projected.astype(f32)]
    pad x1 -> x0, local copies, waits for them, and re-layouts: 1.25 us -> none  [body(): route_tile = jnp.pad(route, ((0, 7), (0, 128 - bricks)))]
where the time goes in v2:
time: 72.2 us; the launch traced here: 72 us
  Pallas kernels  71.3 us (99%)
    pallas_call x1, Pallas kernels, body(): pl.pallas_call(functools.partial(back_kernel, owners, scenes, cap, split)...  48.8 us
    pallas_call x1, Pallas kernels, body(): pl.pallas_call(functools.partial(halo_kernel, owners), out_shape=[arr(pla...  9.58 us
    pallas_call x1, Pallas kernels, body(): pl.pallas_call(functools.partial(conv_kernel, owners, cap), out_shape=[ar...  9.17 us
    pallas_call x1, Pallas kernels, body(): pl.pallas_call(tail_kernel, grid=(bricks,), out_shape=[arr((27 * channels...  3.78 us

profile of v2, /device:TPU:0, one launch (start us, length us, event | category | flops | bytes accessed | tf_op | source)
XLA Modules:
  0.0 72.0 jit_solution(6357459307105184132)
XLA Ops:
  0.6 9.6 %shard_map.85 = (bf16[4,8,8,128]{3,2,1,0:T(8,128)(2,1)}, bf16[4,8,8,128]{3,2,1,0:T(8,128)(2,1)}, s32[4,1,4]{2,1,0:T(1,128)}) custom-call(bf16[4,8,8,8,128]{4,3,2,1,0:T(8,128)(2,1)} %bitcast.6, s32[1,4]{1,0:T(1,128)} %route.1), custom_call_target="tpu_custom_call" | custom-call | tf_op jit(solution)/shard_map/pallas_call | solution.py:416
  10.2 9.2 %shard_map.86 = (f32[4,512,128]{2,1,0:T(8,128)}, bf16[8,512,128]{2,1,0:T(8,128)(2,1)}, bf16[4,640,1152]{2,1,0:T(8,128)(2,1)}, s32[3,8]{1,0:T(4,128)}) custom-call(s32[4,6]{1,0:T(4,128)} %bitcast.10, s32[4,1,4]{2,1,0:T(1,128)} %get-tuple-element.16.routes, bf16[4,8,8,8,128]{4,3,2,1,0:T(8,128)(2,1)} %bitcast.7, ...), custom_call_target="tpu_custom_call" | custom-call | tf_op jit(solution)/shard_map/pallas_call | solution.py:426
  19.4 48.8 %shard_map.87 = (bf16[4,512,128]{2,1,0:T(8,128)(2,1)}, bf16[3584,128]{1,0:T(8,128)(2,1)}, bf16[128,128]{1,0:T(8,128)(2,1)}) custom-call(s32[3,8]{1,0:T(4,128)} %get-tuple-element.19.tables, f32[4,512,128]{2,1,0:T(8,128)} %get-tuple-element.20.taps, bf16[8,512,128]{2,1,0:T(8,128)(2,1)} %get-tuple-element.21.slots, bf16[128,128]{1,0:T(8,128)(2,1)} %projection.1, ...), custom_call_target="tpu_custom_call" | custom-call | tf_op jit(solution)/shard_map/pallas_call | solution.py:455
  68.2 3.8 %shard_map.88 = (f32[3456,128]{1,0:T(8,128)}, f32[128,128]{1,0:T(8,128)}, bf16[4,512,128]{2,1,0:T(8,128)(2,1)}) custom-call(bf16[3584,128]{1,0:T(8,128)(2,1)} %get-tuple-element.23.summed, bf16[128,128]{1,0:T(8,128)(2,1)} %get-tuple-element.24.projected, bf16[4,512,128]{2,1,0:T(8,128)(2,1)} %get-tuple-element.25.acts), custom_call_target="tpu_custom_call" | custom-call | tf_op jit(solution)/shard_map/pallas_call | solution.py:488

commit v3 on v2

--- a/solution.py
+++ b/solution.py
@@ -20,135 +20,6 @@
     return pltpu.CompilerParams(
         vmem_limit_bytes=LIMIT, collective_id=collective, has_side_effects=True
     )
-
-
-def halo_kernel(owners, feats, route, before, after, routes, s_up, r_up, s_dn, r_dn, s_rt, r_rt):
-    me = lax.axis_index("brick")
-    barrier = pltpu.get_barrier_semaphore()
-    for k in range(1, owners):
-        pl.semaphore_signal(
-            barrier, inc=1, device_id={"brick": lax.rem(me + k, owners)}, device_id_type=MESH
-        )
-    pl.semaphore_wait(barrier, owners - 1)
-    up = pltpu.make_async_remote_copy(
-        src_ref=feats.at[:, 7], dst_ref=before, send_sem=s_up, recv_sem=r_up,
-        device_id={"brick": lax.rem(me + 1, owners)}, device_id_type=MESH,
-    )
-    down = pltpu.make_async_remote_copy(
-        src_ref=feats.at[:, 0], dst_ref=after, send_sem=s_dn, recv_sem=r_dn,
-        device_id={"brick": lax.rem(me + owners - 1, owners)}, device_id_type=MESH,
-    )
-    up.start()
-    down.start()
-    sends = []
-    for k in range(1, owners):
-        copy = pltpu.make_async_remote_copy(
-            src_ref=route, dst_ref=routes.at[me], send_sem=s_rt.at[k], recv_sem=r_rt.at[k],
-            device_id={"brick": lax.rem(me + k, owners)}, device_id_type=MESH,
-        )
-        copy.start()
-        sends.append(copy)
-    routes[me] = route[...]
-    for copy in sends:
-        copy.wait()
-    up.wait()
-    down.wait()
-
-
-def conv_kernel(
-    owners, cap, nb, routes, feats, before, after, weights,
-    taps, slots, z, tables, full, plus, minus, ext, wide, links,
-):
-    me = lax.axis_index("brick")
-    bricks = feats.shape[0]
-    start = me * bricks
-    for r in range(bricks):
-        up = nb[r, 0]
-        dn = nb[r, 1]
-        links[r, 0] = jnp.where(up >= 0, up - start, 2 * bricks)
-        links[r, 1] = jnp.where(
-            dn >= 0, jnp.where(dn >= start, dn - start, dn - start + 2 * bricks), 2 * bricks
-        )
-        for e in range(2, 6):
-            links[r, e] = jnp.where(nb[r, e] >= 0, nb[r, e] - start, bricks)
-    for e in range(6):
-        links[bricks, e] = jnp.int32(2 * bricks if e < 2 else bricks)
-    for i in range(owners * cap):
-        tables[2, i] = jnp.int32(0)
-
-    def one_owner(s, carry):
-        targets = [lax.div(routes[s, 0, r], bricks) for r in range(bricks)]
-        for r in range(bricks):
-            count = jnp.int32(0)
-            for e in range(r):
-                count = count + jnp.where(targets[e] == targets[r], 1, 0)
-
-            @pl.when(s == me)
-            def _():
-                tables[0, r] = targets[r] * cap + count
-
-            @pl.when(targets[r] == me)
-            def _():
-                row = lax.rem(routes[s, 0, r], bricks)
-                tables[1, row] = s * cap + count
-                tables[2, s * cap + count] = row
-
-        return carry
-
-    lax.fori_loop(0, owners, one_owner, 0)
-
-    for p in range(3):
-        wide[:, p * 128 : (p + 1) * 128] = weights[9 * p : 9 * p + 9].reshape(1152, 128)
-    full[:bricks] = feats[...].astype(f32)
-    full[bricks] = jnp.zeros(full.shape[1:], f32)
-    plus[:bricks] = feats[:, 0].astype(f32)
-    plus[bricks : 2 * bricks] = after[...].astype(f32)
-    plus[2 * bricks] = jnp.zeros(plus.shape[1:], f32)
-    minus[:bricks] = feats[:, 7].astype(f32)
-    minus[bricks : 2 * bricks] = before[...].astype(f32)
-    minus[2 * bricks] = jnp.zeros(minus.shape[1:], f32)
-
-    def shifted(t, inside, side):
-        if t == 0:
-            return inside
-        axis = inside.ndim - 2
-        place = lax.broadcasted_iota(jnp.int32, inside.shape, axis)
-        joined = jnp.where(place == (0 if t > 0 else 7), side, inside)
-        return pltpu.roll(joined, 7 if t > 0 else 1, axis)
-
-    def one_brick(r, carry):
-        r1 = {0: r, 1: links[r, 4], -1: links[r, 5]}
-        r2 = {}
-        for t in (-1, 0, 1):
-            r2[0, t] = r1[t]
-            r2[1, t] = links[r1[t], 2]
-            r2[-1, t] = links[r1[t], 3]
-        r3 = {}
-        for q, t in r2:
-            r3[1, q, t] = links[r2[q, t], 0]
-            r3[-1, q, t] = links[r2[q, t], 1]
-        for t in (-1, 0, 1):
-            ext[t + 1, 1:9, 1:9] = shifted(t, full[r], full[r1[t]])
-            ext[t + 1, 1:9, 0] = shifted(t, full[r2[-1, 0], :, 7], full[r2[-1, t], :, 7])
-            ext[t + 1, 1:9, 9] = shifted(t, full[r2[1, 0], :, 0], full[r2[1, t], :, 0])
-            for p, table in ((-1, minus), (1, plus)):
-                a = 0 if p < 0 else 9
-                ext[t + 1, a, 1:9] = shifted(t, table[r3[p, 0, 0]], table[r3[p, 0, t]])
-                ext[t + 1, a, 0] = shifted(t, table[r3[p, -1, 0], 7], table[r3[p, -1, t], 7])
-                ext[t + 1, a, 9] = shifted(t, table[r3[p, 1, 0], 0], table[r3[p, 1, t], 0])
-        for q in range(3):
-            for t in range(3):
-                lane = (3 * q + t) * 128
-                z[r, :, lane : lane + 128] = (
-                    ext[t, :, q : q + 8].reshape(640, 128).astype(bf16)
-                )
-        product = jnp.dot(z[r], wide[...], preferred_element_type=f32)
-        total = product[0:512, 0:128] + product[64:576, 128:256] + product[128:640, 256:384]
-        taps[r] = total
-        slots[tables[0, r]] = (total / (1.0 + jnp.exp(-total))).astype(bf16)
-        return carry
-
-    lax.fori_loop(0, bricks, one_brick, 0)
 
 
 def reduce_part(grads, out, base, outer, inner, rx1, part, rx2, sems, started):
@@ -234,18 +105,27 @@
     return scatter, forward, finish, gather, end, order
 
 
-def back_kernel(
-    owners, scenes, cap, split, tables, taps, slots, projection, cotangent, z_far,
+def shifted(t, inside, side):
+    if t == 0:
+        return inside
+    axis = inside.ndim - 2
+    place = lax.broadcasted_iota(jnp.int32, inside.shape, axis)
+    joined = jnp.where(place == (0 if t > 0 else 7), side, inside)
+    return pltpu.roll(joined, 7 if t > 0 else 1, axis)
+
+
+def whole_kernel(
+    owners, scenes, cap, split, nb, route, feats, weights, projection, cotangent,
     acts, out, proj,
+    before, after, routes, routes_s, links, tables, full, plus, minus, ext, wide, taps, tiles, slots,
     z, slope, skip, factor, lifted, arrived, back, spread, total, grads, rx, part,
-    rx2a, rx2b, rx1b, partb, z_sem, s_sem, r_sem, s_bk, r_bk, *rest,
+    rx2a, rx2b, rx1b, partb, s_up, r_up, s_dn, r_dn, s_rt, r_rt, rs_sem,
+    s_sem, r_sem, s_bk, r_bk, *rest,
 ):
     me = lax.axis_index("brick")
     scene = lax.axis_index("dp")
     section = lax.axis_index("section")
-    bricks = taps.shape[0]
-    z_copy = pltpu.make_async_copy(z_far, z, z_sem)
-    z_copy.start()
+    bricks = feats.shape[0]
     barrier = pltpu.get_barrier_semaphore()
     for d in range(owners):
         pl.semaphore_signal(
@@ -259,7 +139,146 @@
         pl.semaphore_signal(
             barrier, inc=1, device_id={"dp": lax.rem(scene + k, scenes)}, device_id_type=MESH
         )
+    routes[me] = route[...]
+    start = me * bricks
+
+    def inside(index, last):
+        return jnp.minimum(jnp.maximum(index, 0), last)
+
+    for r in range(bricks):
+        up = nb[r, 0]
+        dn = nb[r, 1]
+        links[r, 0] = inside(jnp.where(up >= 0, up - start, 2 * bricks), 2 * bricks)
+        back_row = jnp.where(dn >= start, dn - start, dn - start + 2 * bricks)
+        links[r, 1] = inside(jnp.where(dn >= 0, back_row, 2 * bricks), 2 * bricks)
+        for e in range(2, 6):
+            links[r, e] = inside(jnp.where(nb[r, e] >= 0, nb[r, e] - start, bricks), bricks)
+    for e in range(6):
+        links[bricks, e] = jnp.int32(2 * bricks if e < 2 else bricks)
+    full[:bricks] = feats[...].astype(f32)
+    full[bricks] = jnp.zeros(full.shape[1:], f32)
+    for p in range(3):
+        wide[:, p * 128 : (p + 1) * 128] = weights[9 * p : 9 * p + 9].reshape(1152, 128)
     pl.semaphore_wait(barrier, 2 * owners - 1 + scenes - 1)
+
+    halo = [
+        pltpu.make_async_remote_copy(
+            src_ref=feats.at[:, 7], dst_ref=before, send_sem=s_up, recv_sem=r_up,
+            device_id={"brick": lax.rem(me + 1, owners)}, device_id_type=MESH,
+        ),
+        pltpu.make_async_remote_copy(
+            src_ref=feats.at[:, 0], dst_ref=after, send_sem=s_dn, recv_sem=r_dn,
+            device_id={"brick": lax.rem(me + owners - 1, owners)}, device_id_type=MESH,
+        ),
+    ]
+    for k in range(1, owners):
+        halo.append(
+            pltpu.make_async_remote_copy(
+                src_ref=route, dst_ref=routes.at[me], send_sem=s_rt.at[k], recv_sem=r_rt.at[k],
+                device_id={"brick": lax.rem(me + k, owners)}, device_id_type=MESH,
+            )
+        )
+    for copy in halo:
+        copy.start()
+
+    def chains(r):
+        r1 = {0: r, 1: links[r, 4], -1: links[r, 5]}
+        r2 = {}
+        for t in (-1, 0, 1):
+            r2[0, t] = r1[t]
+            r2[1, t] = links[r1[t], 2]
+            r2[-1, t] = links[r1[t], 3]
+        return r1, r2
+
+    def inner_planes(r, carry):
+        r1, r2 = chains(r)
+        for t in (-1, 0, 1):
+            ext[t + 1, 1:9, 1:9] = shifted(t, full[r], full[r1[t]])
+            ext[t + 1, 1:9, 0] = shifted(t, full[r2[-1, 0], :, 7], full[r2[-1, t], :, 7])
+            ext[t + 1, 1:9, 9] = shifted(t, full[r2[1, 0], :, 0], full[r2[1, t], :, 0])
+        for q in range(3):
+            for t in range(3):
+                lane = (3 * q + t) * 128
+                z[r, 64:576, lane : lane + 128] = (
+                    ext[t, 1:9, q : q + 8].reshape(512, 128).astype(bf16)
+                )
+        return carry
+
+    lax.fori_loop(0, bricks, inner_planes, 0)
+    plus[:bricks] = feats[:, 0].astype(f32)
+    plus[2 * bricks] = jnp.zeros(plus.shape[1:], f32)
+    minus[:bricks] = feats[:, 7].astype(f32)
+    minus[2 * bricks] = jnp.zeros(minus.shape[1:], f32)
+    for copy in halo:
+        copy.wait_recv()
+    route_copy = pltpu.make_async_copy(routes, routes_s, rs_sem)
+    route_copy.start()
+    plus[bricks : 2 * bricks] = after[...].astype(f32)
+    minus[bricks : 2 * bricks] = before[...].astype(f32)
+
+    def outer_planes(r, carry):
+        r1, r2 = chains(r)
+        for p, table in ((-1, minus), (1, plus)):
+            a = 0 if p < 0 else 9
+            r3 = {place: links[r2[place], 0 if p > 0 else 1] for place in r2}
+            for t in (-1, 0, 1):
+                ext[t + 1, a, 1:9] = shifted(t, table[r3[0, 0]], table[r3[0, t]])
+                ext[t + 1, a, 0] = shifted(t, table[r3[-1, 0], 7], table[r3[-1, t], 7])
+                ext[t + 1, a, 9] = shifted(t, table[r3[1, 0], 0], table[r3[1, t], 0])
+            for q in range(3):
+                for t in range(3):
+                    lane = (3 * q + t) * 128
+                    z[r, 64 * a : 64 * a + 64, lane : lane + 128] = (
+                        ext[t, a, q : q + 8].reshape(64, 128).astype(bf16)
+                    )
+        product = jnp.dot(z[r], wide[...], preferred_element_type=f32)
+        total_taps = product[0:512, 0:128] + product[64:576, 128:256] + product[128:640, 256:384]
+        taps[r] = total_taps
+        tiles[r] = (total_taps / (1.0 + jnp.exp(-total_taps))).astype(bf16)
+        return carry
+
+    lax.fori_loop(0, bricks, outer_planes, 0)
+    route_copy.wait()
+
+    def places(s):
+        targets = [inside(lax.div(routes_s[s, 0, r], bricks), owners - 1) for r in range(bricks)]
+        counts = []
+        for r in range(bricks):
+            count = jnp.int32(0)
+            for e in range(r):
+                count = count + jnp.where(targets[e] == targets[r], 1, 0)
+            counts.append(jnp.minimum(count, cap - 1))
+        return targets, counts
+
+    targets, counts = places(me)
+    mine = [targets[r] * cap + counts[r] for r in range(bricks)]
+    for r in range(bricks):
+        tables[0, r] = mine[r]
+    for i in range(owners * cap):
+        which = jnp.int32(0)
+        for r in range(1, bricks):
+            which = jnp.where(mine[r] == i, r, which)
+        tables[3, i] = which
+
+    def one_owner(s, found):
+        targets, counts = places(s)
+        found = list(found)
+        rows = [inside(lax.rem(routes_s[s, 0, r], bricks), bricks - 1) for r in range(bricks)]
+        for r in range(bricks):
+            for row in range(bricks):
+                hit = jnp.logical_and(targets[r] == me, rows[r] == row)
+                found[row] = jnp.where(hit, s * cap + counts[r], found[row])
+        for j in range(cap):
+            tag = jnp.int32(0)
+            for r in range(bricks):
+                hit = jnp.logical_and(targets[r] == me, counts[r] == j)
+                tag = jnp.where(hit, rows[r], tag)
+            tables[2, s * cap + j] = tag
+        return tuple(found)
+
+    found = lax.fori_loop(0, owners, one_owner, (jnp.int32(0),) * bricks)
+    for row in range(bricks):
+        tables[1, row] = found[row]
 
     pieces = s_sem.shape[0]
     height = 512 // pieces
@@ -278,6 +297,13 @@
     @pl.when(section == 0)
     def _():
         for c in range(pieces):
+            span = slice(c * height, (c + 1) * height)
+
+            def fill(i, carry):
+                slots[i, span] = tiles[tables[3, i], span]
+                return carry
+
+            lax.fori_loop(0, owners * cap, fill, 0)
             for k in order:
                 move(c, k, slots, s_sem, r_sem).start()
         skip[...] = jnp.zeros(skip.shape, skip.dtype)
@@ -332,7 +358,6 @@
             for k in order:
                 move(c, k, back, s_bk, r_bk).start()
 
-    z_copy.wait()
     spread[...] = jnp.zeros(spread.shape, bf16)
     total[...] = jnp.zeros(total.shape, f32)
 
@@ -398,52 +423,47 @@
 
     for copy in started:
         copy.wait_send()
-
-
-def tail_kernel(summed, projected, acts, weight_out, proj_out, acts_out):
-    weight_out[...] = summed[...].astype(f32)
-    proj_out[...] = projected[...].astype(f32)
-    acts_out[...] = acts[...]
+    for copy in halo:
+        copy.wait_send()
+
+
+def tail_kernel(
+    summed, projected, acts, weight_out, proj_out, acts_out,
+    narrow, wider, proj_in, proj_wide, in_sem, out_sem, p_in, p_out, a_sem,
+):
+    pieces, rows = narrow.shape[:2]
+    acts_copy = pltpu.make_async_copy(acts, acts_out, a_sem)
+    fetch, store = [], []
+    for c in range(pieces):
+        span = pl.ds(c * rows, rows)
+        fetch.append(pltpu.make_async_copy(summed.at[span], narrow.at[c], in_sem.at[c]))
+        store.append(pltpu.make_async_copy(wider.at[c], weight_out.at[span], out_sem.at[c]))
+        fetch[c].start()
+    proj_fetch = pltpu.make_async_copy(projected, proj_in, p_in)
+    proj_fetch.start()
+    acts_copy.start()
+    for c in range(pieces):
+        fetch[c].wait()
+        wider[c] = narrow[c].astype(f32)
+        store[c].start()
+    proj_fetch.wait()
+    proj_wide[...] = proj_in[...].astype(f32)
+    proj_store = pltpu.make_async_copy(proj_wide, proj_out, p_out)
+    proj_store.start()
+    for copy in store:
+        copy.wait()
+    proj_store.wait()
+    acts_copy.wait()
 
 
 def body(features, weights, projection, cotangent, neighbours, route):
     bricks, channels = features.shape[2], features.shape[-1]
     owners, scenes = lax.axis_size("brick"), lax.axis_size("dp")
     cap = max(2, 3 * bricks // (2 * owners))
+    count = owners * cap
     feats = features[0, 0].reshape(bricks, 8, 8, 8, channels)
-    dma, arr = pltpu.SemaphoreType.DMA, jax.ShapeDtypeStruct
+    dma, arr, vm = pltpu.SemaphoreType.DMA, jax.ShapeDtypeStruct, pltpu.VMEM
     plane = (bricks, 8, 8, channels)
-    before, after, routes = pl.pallas_call(
-        functools.partial(halo_kernel, owners),
-        out_shape=[arr(plane, bf16), arr(plane, bf16), arr((owners, 1, bricks), jnp.int32)],
-        in_specs=[VM, VM],
-        out_specs=[VM, VM, VM],
-        scratch_shapes=[dma, dma, dma, dma, dma((owners,)), dma((owners,))],
-        compiler_params=params(0),
-    )(feats, route)
-
-    count = owners * cap
-    taps, slots, z, tables = pl.pallas_call(
-        functools.partial(conv_kernel, owners, cap),
-        out_shape=[
-            arr((bricks, 512, channels), f32),
-            arr((count, 512, channels), bf16),
-            arr((bricks, 640, 9 * channels), bf16),
-            arr((3, max(count, bricks)), jnp.int32),
-        ],
-        in_specs=[SM, SM, VM, VM, VM, VM],
-        out_specs=[VM, VM, VM, SM],
-        scratch_shapes=[
-            pltpu.VMEM((bricks + 1, 8, 8, 8, channels), f32),
-            pltpu.VMEM((2 * bricks + 1, 8, 8, channels), f32),
-            pltpu.VMEM((2 * bricks + 1, 8, 8, channels), f32),
-            pltpu.VMEM((3, 10, 10, 8, channels), f32),
-            pltpu.VMEM((9 * channels, 3 * channels), bf16),
-            pltpu.SMEM((bricks + 1, 6), jnp.int32),
-        ],
-        compiler_params=params(),
-    )(neighbours[0, 0], routes, feats, before, after, weights[0])
-
     tile = (bricks, 512, channels)
     unit = 16 * owners * scenes
     units = -(-28 * channels // unit)
@@ -451,16 +471,26 @@
     split = (2 * units + 2) // 3 * unit
     height_a, height_b = split // (owners * scenes), (total - split) // (owners * scenes)
     pieces = 4
-    vm = pltpu.VMEM
+    anywhere = pl.BlockSpec(memory_space=pl.ANY)
     acts, summed, projected = pl.pallas_call(
-        functools.partial(back_kernel, owners, scenes, cap, split),
+        functools.partial(whole_kernel, owners, scenes, cap, split),
         out_shape=[
             arr(tile, bf16), arr((total, channels), bf16), arr((channels, channels), bf16)
         ],
-        in_specs=[SM, VM, VM, VM, VM, pl.BlockSpec(memory_space=pl.ANY)],
+        in_specs=[SM, VM, VM, VM, VM, VM],
         out_specs=[VM, VM, VM],
         scratch_shapes=[
-            vm(z.shape, bf16), vm(tile, bf16), vm(tile, bf16), vm(tile, f32), vm(tile, bf16),
+            vm(plane, bf16), vm(plane, bf16), vm((owners, 1, bricks), jnp.int32),
+            pltpu.SMEM((owners, 1, bricks), jnp.int32), pltpu.SMEM((bricks + 1, 6), jnp.int32),
+            pltpu.SMEM((4, max(count, bricks)), jnp.int32),
+            vm((bricks + 1, 8, 8, 8, channels), f32),
+            vm((2 * bricks + 1, 8, 8, channels), f32),
+            vm((2 * bricks + 1, 8, 8, channels), f32),
+            vm((3, 10, 10, 8, channels), f32),
+            vm((9 * channels, 3 * channels), bf16),
+            vm(tile, f32), vm(tile, bf16), vm((count, 512, channels), bf16),
+            vm((bricks, 640, 9 * channels), bf16),
+            vm(tile, bf16), vm(tile, bf16), vm(tile, f32), vm(tile, bf16),
             [vm((count, 512 // pieces, channels), bf16) for _ in range(pieces)],
             vm((count, 512, channels), bf16),
             vm((640, 3 * channels), bf16), vm((9 * channels, 3 * channels), f32),
@@ -471,7 +501,7 @@
             vm((owners, height_b, channels), bf16),
             vm((owners, scenes, height_b, channels), bf16),
             vm((owners, height_b, channels), bf16),
-            dma,
+            dma, dma, dma, dma, dma((owners,)), dma((owners,)), dma,
             *[dma((pieces, owners)) for _ in range(4)],
             dma((scenes, owners)), dma((scenes, owners)),
             *[dma((scenes,)) for _ in range(4)],
@@ -481,25 +511,20 @@
             dma((owners, scenes)), dma((owners, scenes)),
             dma, dma,
         ],
-        compiler_params=params(1),
-    )(tables, taps, slots, projection, cotangent[0, 0], z)
-
-    piece = 27 * channels // bricks
+        compiler_params=params(0),
+    )(neighbours[0, 0], route, feats, weights[0], projection, cotangent[0, 0])
+
     weight_sum, projection_sum, acts = pl.pallas_call(
         tail_kernel,
-        grid=(bricks,),
         out_shape=[
             arr((27 * channels, channels), f32), arr((channels, channels), f32), arr(tile, bf16)
         ],
-        in_specs=[
-            pl.BlockSpec((piece, channels), lambda i: (i, 0)),
-            pl.BlockSpec((channels, channels), lambda i: (0, 0)),
-            pl.BlockSpec((1, 512, channels), lambda i: (i, 0, 0)),
-        ],
-        out_specs=[
-            pl.BlockSpec((piece, channels), lambda i: (i, 0)),
-            pl.BlockSpec((channels, channels), lambda i: (0, 0)),
-            pl.BlockSpec((1, 512, channels), lambda i: (i, 0, 0)),
+        in_specs=[anywhere] * 3,
+        out_specs=[anywhere] * 3,
+        scratch_shapes=[
+            vm((3, 9 * channels, channels), bf16), vm((3, 9 * channels, channels), f32),
+            vm((channels, channels), bf16), vm((channels, channels), f32),
+            dma((3,)), dma((3,)), dma, dma, dma,
         ],
         compiler_params=params(),
     )(summed, projected, acts)

time: 72.2 us -> 78.1 us (1.082)
  Pallas kernels: 71.3 us -> 77.3 us
    pallas_call x4 -> x2, Pallas kernels: 71.3 us -> 77.3 us  [the longest x1 60.2 us: body(): pl.pallas_call(functools.partial(whole_kernel, owners, scenes, cap, split...]
where the time goes in v3:
time: 78.1 us; the launch traced here: 77.9 us
  Pallas kernels  77.3 us (99%)
    pallas_call x1, Pallas kernels, body(): pl.pallas_call(functools.partial(whole_kernel, owners, scenes, cap, split...  60.2 us
    pallas_call x1, Pallas kernels, body(): pl.pallas_call(tail_kernel, out_shape=[arr((27 * channels, channels), f32...  17.1 us

profile of v3, /device:TPU:0, one launch (start us, length us, event | category | flops | bytes accessed | tf_op | source)
XLA Modules:
  0.0 77.9 jit_solution(12780730547096272033)
XLA Ops:
  0.6 60.2 %shard_map.85 = (bf16[4,512,128]{2,1,0:T(8,128)(2,1)}, bf16[3584,128]{1,0:T(8,128)(2,1)}, bf16[128,128]{1,0:T(8,128)(2,1)}) custom-call(s32[4,6]{1,0:T(4,128)} %bitcast.9, s32[1,4]{1,0:T(1,128)} %route.1, bf16[4,8,8,8,128]{4,3,2,1,0:T(8,128)(2,1)} %bitcast.7, bf16[27,128,128]{2,1,0:T(8,128)(2,1)} %bitcast.6, bf16[128,128]{1,0:T(8,128)(2,1)} %projection.1, ...), custom_call_target="tpu_custom_call" | custom-call | tf_op jit(solution)/shard_map/pallas_call | solution.py:475
  60.9 17.1 %shard_map.86 = (f32[3456,128]{1,0:T(8,128)}, f32[128,128]{1,0:T(8,128)}, bf16[4,512,128]{2,1,0:T(8,128)(2,1)}) custom-call(bf16[3584,128]{1,0:T(8,128)(2,1)} %get-tuple-element.9.summed, bf16[128,128]{1,0:T(8,128)(2,1)} %get-tuple-element.10.projected, bf16[4,512,128]{2,1,0:T(8,128)(2,1)} %get-tuple-element.11.acts), custom_call_target="tpu_custom_call" | custom-call | tf_op jit(solution)/shard_map/pallas_call | solution.py:517

commit v4 on v3

--- a/solution.py
+++ b/solution.py
@@ -115,11 +115,10 @@
 
 
 def whole_kernel(
-    owners, scenes, cap, split, nb, route, feats, weights, projection, cotangent,
-    acts, out, proj,
+    owners, scenes, cap, cuts, nb, route, feats, weights, projection, cotangent,
+    acts, out,
     before, after, routes, routes_s, links, tables, full, plus, minus, ext, wide, taps, tiles, slots,
-    z, slope, skip, factor, lifted, arrived, back, spread, total, grads, rx, part,
-    rx2a, rx2b, rx1b, partb, s_up, r_up, s_dn, r_dn, s_rt, r_rt, rs_sem,
+    z, slope, skip, factor, lifted, arrived, back, spread, grads, handed, landing, s_up, r_up, s_dn, r_dn, s_rt, r_rt, rs_sem,
     s_sem, r_sem, s_bk, r_bk, *rest,
 ):
     me = lax.axis_index("brick")
@@ -359,64 +358,74 @@
                 move(c, k, back, s_bk, r_bk).start()
 
     spread[...] = jnp.zeros(spread.shape, bf16)
-    total[...] = jnp.zeros(total.shape, f32)
-
-    def one(r, acc):
-        for p in range(3):
-            spread[p * 64 : p * 64 + 512, p * 128 : (p + 1) * 128] = slope[r]
-        total[...] += lax.dot_general(
-            z[r], spread[...], (((0,), (0,)), ((), ())), preferred_element_type=f32
-        )
-        return acc + lax.dot_general(
-            skip[r], slope[r], (((0,), (0,)), ((), ())), preferred_element_type=f32
-        )
-
-    projected = lax.fori_loop(0, bricks, one, jnp.zeros((128, 128), f32))
     for p in range(3):
-        grads[1152 * p : 1152 * (p + 1)] = total[:, p * 128 : (p + 1) * 128].astype(bf16)
-    grads[3456:3584] = projected.astype(bf16)
+        spread[:, p * 64 : p * 64 + 512, p * 128 : (p + 1) * 128] = slope[...]
+    hand = pltpu.make_async_remote_copy(
+        src_ref=grads.at[pl.ds(3456, 128)], dst_ref=handed, send_sem=rest[0], recv_sem=rest[1],
+        device_id={"section": 1 - section}, device_id_type=MESH,
+    )
+
+    @pl.when(section == 1)
+    def _():
+        grads[3456:3584] = lax.dot_general(
+            skip[...].reshape(bricks * 512, 128), slope[...].reshape(bricks * 512, 128),
+            (((0,), (0,)), ((), ())), preferred_element_type=f32,
+        ).astype(bf16)
+        hand.start()
+
     if grads.shape[0] > 3584:
         grads[3584:] = jnp.zeros((grads.shape[0] - 3584, 128), bf16)
 
     started = []
     on_brick, on_dp = ("brick", owners), ("dp", scenes)
-    one_part = reduce_part(grads, out, 0, on_brick, on_dp, rx, part, rx2a, rest[:8], started)
-    two_part = reduce_part(
-        grads, out, split, on_dp, on_brick, rx1b, partb, rx2b, rest[8:16], started
-    )
-    both = (one_part, two_part)
-    for way in both:
-        way[0]()
+    parts = []
+    for i in range(3):
+        outer, inner = (on_dp, on_brick) if i == 0 else (on_brick, on_dp)
+        parts.append(
+            reduce_part(
+                grads, out, cuts[i], outer, inner, *landing[i],
+                rest[2 + 8 * i : 10 + 8 * i], started,
+            )
+        )
+    for q in range(3):
+        product = lax.dot_general(
+            z[:, :, 384 * q : 384 * (q + 1)].reshape(bricks * 640, 384),
+            spread[...].reshape(bricks * 640, 384),
+            (((0,), (0,)), ((), ())), preferred_element_type=f32,
+        )
+        for p in range(3):
+            first_row = 384 * (3 * q + p)
+            grads[first_row : first_row + 384] = product[:, p * 128 : (p + 1) * 128].astype(bf16)
+        if q == 2:
+
+            @pl.when(section == 0)
+            def _():
+                hand.wait_recv()
+                grads[3456:3584] = handed[...]
+
+        parts[q][0]()
     for i in range(max(owners, scenes)):
-        for way in both:
+        for way in parts:
             if i < len(way[5]):
                 way[1](way[5][i])
-    for way in both:
+    for way in parts:
         way[2]()
     for i in range(1, max(owners, scenes)):
-        for way in both:
+        for way in parts:
             if i < len(way[5]):
                 way[3](i)
-    for way in both:
+    for way in parts:
         way[4]()
-    s5, r5 = rest[16:18]
-    last_copy = pltpu.make_async_remote_copy(
-        src_ref=out.at[pl.ds(3456, 128)], dst_ref=proj, send_sem=s5, recv_sem=r5,
-        device_id={"section": 1 - section}, device_id_type=MESH,
-    )
 
     @pl.when(section == 1)
     def _():
-        last_copy.start()
-        proj[...] = out[3456:3584, :]
-        last_copy.wait_send()
+        hand.wait_send()
         for c in range(pieces):
             for k in order:
                 move(c, k, back, s_bk, r_bk).wait_send()
 
     @pl.when(section == 0)
     def _():
-        last_copy.wait_recv()
         for c in range(pieces):
             for k in order:
                 move(c, k, slots, s_sem, r_sem).wait_send()
@@ -428,32 +437,39 @@
 
 
 def tail_kernel(
-    summed, projected, acts, weight_out, proj_out, acts_out,
-    narrow, wider, proj_in, proj_wide, in_sem, out_sem, p_in, p_out, a_sem,
+    summed, acts, weight_out, proj_out, acts_out,
+    narrow, wider, held, in_sem, out_sem, a_in, a_out,
 ):
-    pieces, rows = narrow.shape[:2]
-    acts_copy = pltpu.make_async_copy(acts, acts_out, a_sem)
+    rows = 384
+    hold = pltpu.make_async_copy(acts, held, a_in)
+    keep = pltpu.make_async_copy(held, acts_out, a_out)
     fetch, store = [], []
-    for c in range(pieces):
-        span = pl.ds(c * rows, rows)
-        fetch.append(pltpu.make_async_copy(summed.at[span], narrow.at[c], in_sem.at[c]))
-        store.append(pltpu.make_async_copy(wider.at[c], weight_out.at[span], out_sem.at[c]))
-        fetch[c].start()
-    proj_fetch = pltpu.make_async_copy(projected, proj_in, p_in)
-    proj_fetch.start()
-    acts_copy.start()
-    for c in range(pieces):
-        fetch[c].wait()
-        wider[c] = narrow[c].astype(f32)
-        store[c].start()
-    proj_fetch.wait()
-    proj_wide[...] = proj_in[...].astype(f32)
-    proj_store = pltpu.make_async_copy(proj_wide, proj_out, p_out)
-    proj_store.start()
+    for q in range(3):
+        size = 1152 if q < 2 else 1280
+        span = pl.ds(1152 * q, size)
+        fetch.append(pltpu.make_async_copy(summed.at[span], narrow.at[span], in_sem.at[q]))
+        fetch[q].start()
+    hold.start()
+    for q in range(3):
+        fetch[q].wait()
+        for p in range(3):
+            place = rows * (3 * q + p)
+            wider[place : place + rows] = narrow[place : place + rows].astype(f32)
+            copy = pltpu.make_async_copy(
+                wider.at[pl.ds(place, rows)], weight_out.at[pl.ds(rows * (3 * p + q), rows)],
+                out_sem.at[3 * q + p],
+            )
+            copy.start()
+            store.append(copy)
+    wider[3456:3584] = narrow[3456:3584].astype(f32)
+    copy = pltpu.make_async_copy(wider.at[pl.ds(3456, 128)], proj_out, out_sem.at[9])
+    copy.start()
+    store.append(copy)
+    hold.wait()
+    keep.start()
     for copy in store:
         copy.wait()
-    proj_store.wait()
-    acts_copy.wait()
+    keep.wait()
 
 
 def body(features, weights, projection, cotangent, neighbours, route):
@@ -468,17 +484,26 @@
     unit = 16 * owners * scenes
     units = -(-28 * channels // unit)
     total = units * unit
-    split = (2 * units + 2) // 3 * unit
-    height_a, height_b = split // (owners * scenes), (total - split) // (owners * scenes)
+    cuts = [0, 9 * channels // unit * unit, 18 * channels // unit * unit, total]
+    heights = [(cuts[i + 1] - cuts[i]) // (owners * scenes) for i in range(3)]
+    landing, signals = [], []
+    for i in range(3):
+        n1, n2 = (scenes, owners) if i == 0 else (owners, scenes)
+        landing.append(
+            [
+                vm((n2, n1, heights[i], channels), bf16),
+                vm((n2, heights[i], channels), bf16),
+                vm((n2, heights[i], channels), bf16),
+            ]
+        )
+        signals += [dma((n2, n1))] * 2 + [dma((n2,))] * 4 + [dma((n2, n1))] * 2
     pieces = 4
     anywhere = pl.BlockSpec(memory_space=pl.ANY)
-    acts, summed, projected = pl.pallas_call(
-        functools.partial(whole_kernel, owners, scenes, cap, split),
-        out_shape=[
-            arr(tile, bf16), arr((total, channels), bf16), arr((channels, channels), bf16)
-        ],
+    acts, summed = pl.pallas_call(
+        functools.partial(whole_kernel, owners, scenes, cap, cuts),
+        out_shape=[arr(tile, bf16), arr((total, channels), bf16)],
         in_specs=[SM, VM, VM, VM, VM, VM],
-        out_specs=[VM, VM, VM],
+        out_specs=[VM, VM],
         scratch_shapes=[
             vm(plane, bf16), vm(plane, bf16), vm((owners, 1, bricks), jnp.int32),
             pltpu.SMEM((owners, 1, bricks), jnp.int32), pltpu.SMEM((bricks + 1, 6), jnp.int32),
@@ -493,23 +518,11 @@
             vm(tile, bf16), vm(tile, bf16), vm(tile, f32), vm(tile, bf16),
             [vm((count, 512 // pieces, channels), bf16) for _ in range(pieces)],
             vm((count, 512, channels), bf16),
-            vm((640, 3 * channels), bf16), vm((9 * channels, 3 * channels), f32),
-            vm((total, channels), bf16),
-            vm((scenes, owners, height_a, channels), bf16),
-            vm((scenes, height_a, channels), bf16),
-            vm((scenes, height_a, channels), bf16),
-            vm((owners, height_b, channels), bf16),
-            vm((owners, scenes, height_b, channels), bf16),
-            vm((owners, height_b, channels), bf16),
+            vm((bricks, 640, 3 * channels), bf16),
+            vm((total, channels), bf16), vm((channels, channels), bf16), landing,
             dma, dma, dma, dma, dma((owners,)), dma((owners,)), dma,
             *[dma((pieces, owners)) for _ in range(4)],
-            dma((scenes, owners)), dma((scenes, owners)),
-            *[dma((scenes,)) for _ in range(4)],
-            dma((scenes, owners)), dma((scenes, owners)),
-            dma((owners, scenes)), dma((owners, scenes)),
-            *[dma((owners,)) for _ in range(4)],
-            dma((owners, scenes)), dma((owners, scenes)),
-            dma, dma,
+            dma, dma, *signals,
         ],
         compiler_params=params(0),
     )(neighbours[0, 0], route, feats, weights[0], projection, cotangent[0, 0])
@@ -519,15 +532,14 @@
         out_shape=[
             arr((27 * channels, channels), f32), arr((channels, channels), f32), arr(tile, bf16)
         ],
-        in_specs=[anywhere] * 3,
+        in_specs=[anywhere] * 2,
         out_specs=[anywhere] * 3,
         scratch_shapes=[
-            vm((3, 9 * channels, channels), bf16), vm((3, 9 * channels, channels), f32),
-            vm((channels, channels), bf16), vm((channels, channels), f32),
-            dma((3,)), dma((3,)), dma, dma, dma,
+            vm((28 * channels, channels), bf16), vm((28 * channels, channels), f32),
+            vm(tile, bf16), dma((3,)), dma((10,)), dma, dma,
         ],
         compiler_params=params(),
-    )(summed, projected, acts)
+    )(summed, acts)
     return (
         acts[None, None],
         weight_sum.reshape(1, 27, channels, channels),

time: 78.1 us -> 62.6 us (0.80)
  Pallas kernels: 77.3 us -> 61.8 us
    pallas_call x1, Pallas kernels: 17.1 us -> 2.5 us  [body(): pl.pallas_call(tail_kernel, out_shape=[arr((27 * channels, channels), f32...]
    pallas_call x1, Pallas kernels: 60.2 us -> 59.3 us  [body(): pl.pallas_call(functools.partial(whole_kernel, owners, scenes, cap, cuts)...]
where the time goes in v4:
time: 62.6 us; the launch traced here: 62.4 us
  Pallas kernels  61.8 us (99%)
  between operations  0.64 us (1%)
    pallas_call x1, Pallas kernels, body(): pl.pallas_call(functools.partial(whole_kernel, owners, scenes, cap, cuts)...  59.3 us
    pallas_call x1, Pallas kernels, body(): pl.pallas_call(tail_kernel, out_shape=[arr((27 * channels, channels), f32...  2.5 us

profile of v4, /device:TPU:0, one launch (start us, length us, event | category | flops | bytes accessed | tf_op | source)
XLA Modules:
  0.0 62.4 jit_solution(10333237668064372185)
XLA Ops:
  0.6 59.3 %shard_map.85 = (bf16[4,512,128]{2,1,0:T(8,128)(2,1)}, bf16[3584,128]{1,0:T(8,128)(2,1)}) custom-call(s32[4,6]{1,0:T(4,128)} %bitcast.9, s32[1,4]{1,0:T(1,128)} %route.1, bf16[4,8,8,8,128]{4,3,2,1,0:T(8,128)(2,1)} %bitcast.7, bf16[27,128,128]{2,1,0:T(8,128)(2,1)} %bitcast.6, bf16[128,128]{1,0:T(8,128)(2,1)} %projection.1, bf16[4,512,128]{2,1,0:T(8,128)(2,1)} %bitcast.8), custom_call_target="tpu_custom_call" | custom-call | tf_op jit(solution)/shard_map/pallas_call | solution.py:502
  59.9 2.5 %shard_map.86 = (f32[3456,128]{1,0:T(8,128)}, f32[128,128]{1,0:T(8,128)}, bf16[4,512,128]{2,1,0:T(8,128)(2,1)}) custom-call(bf16[3584,128]{1,0:T(8,128)(2,1)} %get-tuple-element.8.summed, bf16[4,512,128]{2,1,0:T(8,128)(2,1)} %get-tuple-element.9.acts), custom_call_target="tpu_custom_call" | custom-call | tf_op jit(solution)/shard_map/pallas_call | solution.py:530

commit v5 on v4

--- a/solution.py
+++ b/solution.py
@@ -230,10 +230,6 @@
                     z[r, 64 * a : 64 * a + 64, lane : lane + 128] = (
                         ext[t, a, q : q + 8].reshape(64, 128).astype(bf16)
                     )
-        product = jnp.dot(z[r], wide[...], preferred_element_type=f32)
-        total_taps = product[0:512, 0:128] + product[64:576, 128:256] + product[128:640, 256:384]
-        taps[r] = total_taps
-        tiles[r] = (total_taps / (1.0 + jnp.exp(-total_taps))).astype(bf16)
         return carry
 
     lax.fori_loop(0, bricks, outer_planes, 0)
@@ -279,6 +275,7 @@
     for row in range(bricks):
         tables[1, row] = found[row]
 
+
     pieces = s_sem.shape[0]
     height = 512 // pieces
 
@@ -292,11 +289,22 @@
         )
 
     order = [k for k in range(1, owners)] + [0]
-
-    @pl.when(section == 0)
-    def _():
-        for c in range(pieces):
-            span = slice(c * height, (c + 1) * height)
+    for c in range(pieces):
+        span = slice(c * height, (c + 1) * height)
+        chunk_taps = jnp.zeros((bricks * height, 128), f32)
+        for p in range(3):
+            low = c * height + 64 * p
+            chunk_taps = chunk_taps + jnp.dot(
+                z[:, low : low + height].reshape(bricks * height, 1152),
+                wide[:, p * 128 : (p + 1) * 128],
+                preferred_element_type=f32,
+            )
+        taps[:, span] = chunk_taps.reshape(bricks, height, 128)
+
+        @pl.when(section == 0)
+        def _():
+            v = taps[:, span]
+            tiles[:, span] = (v / (1.0 + jnp.exp(-v))).astype(bf16)
 
             def fill(i, carry):
                 slots[i, span] = tiles[tables[3, i], span]
@@ -305,7 +313,9 @@
             lax.fori_loop(0, owners * cap, fill, 0)
             for k in order:
                 move(c, k, slots, s_sem, r_sem).start()
-        skip[...] = jnp.zeros(skip.shape, skip.dtype)
+
+    @pl.when(section == 0)
+    def _():
 
         def gate(r, carry):
             v = taps[r]

time: 62.6 us -> 61.4 us (0.981)
  Pallas kernels: 61.8 us -> 60.6 us
    pallas_call x1, Pallas kernels: 59.3 us -> 58.1 us  [body(): pl.pallas_call(functools.partial(whole_kernel, owners, scenes, cap, cuts)...]
where the time goes in v5:
time: 61.4 us; the launch traced here: 61.3 us
  Pallas kernels  60.6 us (99%)
  between operations  0.64 us (1%)
    pallas_call x1, Pallas kernels, body(): pl.pallas_call(functools.partial(whole_kernel, owners, scenes, cap, cuts)...  58.1 us
    pallas_call x1, Pallas kernels, body(): pl.pallas_call(tail_kernel, out_shape=[arr((27 * channels, channels), f32...  2.5 us

profile of v5, /device:TPU:0, one launch (start us, length us, event | category | flops | bytes accessed | tf_op | source)
XLA Modules:
  0.0 61.3 jit_solution(10330318132100847063)
XLA Ops:
  0.6 58.1 %shard_map.85 = (bf16[4,512,128]{2,1,0:T(8,128)(2,1)}, bf16[3584,128]{1,0:T(8,128)(2,1)}) custom-call(s32[4,6]{1,0:T(4,128)} %bitcast.9, s32[1,4]{1,0:T(1,128)} %route.1, bf16[4,8,8,8,128]{4,3,2,1,0:T(8,128)(2,1)} %bitcast.7, bf16[27,128,128]{2,1,0:T(8,128)(2,1)} %bitcast.6, bf16[128,128]{1,0:T(8,128)(2,1)} %projection.1, bf16[4,512,128]{2,1,0:T(8,128)(2,1)} %bitcast.8), custom_call_target="tpu_custom_call" | custom-call | tf_op jit(solution)/shard_map/pallas_call | solution.py:512
  58.8 2.5 %shard_map.86 = (f32[3456,128]{1,0:T(8,128)}, f32[128,128]{1,0:T(8,128)}, bf16[4,512,128]{2,1,0:T(8,128)(2,1)}) custom-call(bf16[3584,128]{1,0:T(8,128)(2,1)} %get-tuple-element.8.summed, bf16[4,512,128]{2,1,0:T(8,128)(2,1)} %get-tuple-element.9.acts), custom_call_target="tpu_custom_call" | custom-call | tf_op jit(solution)/shard_map/pallas_call | solution.py:540
